TPU v7x, 512 devices: a whole 4x8x8 slice. The times are simulated.
512 devices in a mesh: ctx: 32 (over z, y_lo, core), tp: 4 (over x), var: 4 (over y_hi).
Axes of the slice: x: 4, y: 8 (y_hi: 4, y_lo: 2; y = y_hi * 2 + y_lo), z: 8, core: 2. Of those that a mesh axis runs over, the one named last changes fastest.
Arguments:
- context_kv: bfloat16 [2, 8192, 8192], P(None, ('ctx', 'var'), 'tp'), may hold values from -14 to 14
- queries: bfloat16 [128, 32, 8192], P(('ctx', 'var'), None, 'tp'), may hold values from -14 to 14
- cont_keys: bfloat16 [128, 32, 8192], P(('ctx', 'var'), None, 'tp'), may hold values from -6 to 6
- hyena_inputs: bfloat16 [3, 128, 32, 8192], P(None, ('ctx', 'var'), None, 'tp'), may hold values from -6 to 6
- hyena_state: bfloat16 [128, 8192], P(('ctx', 'var'), 'tp'), may hold values from -6 to 6
- hyena_filter: float32 [8192, 128], P('tp'), may hold values from -0.6 to 0.6
- filter_skip: float32 [8192], P('tp'), may hold values from -3 to 3
- unembed: bfloat16 [8192, 512], P('tp'), may hold values from -21 to 21
- ref_bases: int32 [32], replicated, may hold values from 0 to 3
- variant_pos: int32 [128], P(('ctx', 'var')), may hold values from 0 to 31
- allele_ids: int32 [128], P(('ctx', 'var')), may hold values from 0 to 3
- cont_lengths: int32 [128], P(('ctx', 'var')), may hold values from 16 to 32, as said below
Outputs:
- hyena_out: bfloat16 [128, 32, 8192], P(('ctx', 'var'), None, 'tp')
- log_probs: float32 [128, 32], P(('ctx', 'var'))
- variant_scores: float32 [128], P(('ctx', 'var'))
Inputs may be any that keep to these rules, and one draw needn't show every extreme that they name: `variant_pos`: position of the variant inside its continuation. `allele_ids`: base codes of the alleles. `cont_lengths`: some continuation has 32 scored bases and some has 16.
All inputs are finite; a program needn't handle non-finite values.
Results may differ from a plain program's by a relative error of at most 0.0065.
Values may be sent and summed in bfloat16 or wider, within the bound.
A program may use at most 192 MiB of HBM per device.

v0:
```python
import jax
import jax.numpy as jnp
from jax import lax
from jax.sharding import PartitionSpec as P

HEAD_DIM = 128


BASE_TOKENS = (65, 67, 71, 84)
TAP_BLOCK = 32


def summarize(scores, values):
    maxima = scores.max(-1)
    weights = jnp.exp(scores - maxima[..., None])
    totals = weights.sum(-1)
    numerators = jnp.einsum(
        "rhk,khd->rhd", weights.astype(jnp.bfloat16), values, preferred_element_type=jnp.float32
    ).astype(jnp.bfloat16)
    return (maxima, totals, numerators)


def on_device(
    context_kv,
    queries,
    cont_keys,
    hyena_inputs,
    hyena_state,
    hyena_filter,
    filter_skip,
    unembed,
    ref_bases,
    variant_pos,
    allele_ids,
    cont_lengths,
):
    highest = lax.Precision.HIGHEST
    channels = queries.shape[2]
    positions = queries.shape[1]
    head_count = channels // HEAD_DIM
    vocab_size = unembed.shape[1]
    score_scale = HEAD_DIM ** (-0.5)
    filter_len = hyena_filter.shape[1]
    past_rows = lax.all_gather(hyena_state, ("ctx", "var"), axis=0, tiled=True)
    gate_in = hyena_inputs[0, 0]
    product = (
        hyena_inputs[1, 0].astype(jnp.float32) * hyena_inputs[2, 0].astype(jnp.float32)
    ).astype(jnp.bfloat16)
    sequence = jnp.concatenate([past_rows, product], 0)
    mixed = filter_skip[None, :] * product.astype(jnp.float32)
    for first_tap in range(1, filter_len + 1, TAP_BLOCK):
        last_tap = min(first_tap + TAP_BLOCK, filter_len + 1)
        windows = jnp.stack(
            [
                lax.slice_in_dim(
                    sequence, filter_len - offset, filter_len - offset + positions, axis=0
                )
                for offset in range(first_tap, last_tap)
            ],
            1,
        )
        coeff_block = jnp.transpose(hyena_filter[:, first_tap - 1 : last_tap - 1])
        mixed = mixed + (windows.astype(jnp.float32) * coeff_block[None]).sum(1)
    hyena_row = (gate_in.astype(jnp.float32) * mixed).astype(jnp.bfloat16)
    gathered_kv = lax.all_gather(context_kv, "var", axis=1, tiled=True)
    ctx_keys = gathered_kv[0].reshape(-1, head_count, HEAD_DIM)
    ctx_values = gathered_kv[1].reshape(-1, head_count, HEAD_DIM)
    all_queries = lax.all_gather(queries, "ctx", axis=0, tiled=True)
    ranks = all_queries.shape[0]
    group = min(ranks, max(1, 512 // positions))
    while ranks % group:
        group = group - 1
    blocked = all_queries.reshape(ranks // group, group * positions, head_count, HEAD_DIM)

    def block_partials(block_rows):
        scores = (
            jnp.einsum("rhd,khd->rhk", block_rows, ctx_keys, preferred_element_type=jnp.float32)
            * score_scale
        )
        return summarize(scores, ctx_values)

    maxima, totals, numerators = lax.map(block_partials, blocked)
    maxima = maxima.reshape(ranks, positions, head_count)
    totals = totals.reshape(ranks, positions, head_count)
    numerators = numerators.reshape(ranks, positions, head_count, HEAD_DIM)
    own_queries = queries[0].reshape(positions, head_count, HEAD_DIM)
    own_keys = cont_keys[0].reshape(positions, head_count, HEAD_DIM)
    self_scores = (
        jnp.einsum("thd,shd->ths", own_queries, own_keys, preferred_element_type=jnp.float32)
        * score_scale
    )
    places = jnp.arange(positions)
    causal = places[:, None] >= places[None, :]
    self_scores = jnp.where(causal[:, None, :], self_scores, -jnp.inf)
    self_max, self_total, self_numer = summarize(
        self_scores, hyena_row.reshape(positions, head_count, HEAD_DIM)
    )
    received_numer = lax.all_to_all(numerators, "ctx", split_axis=0, concat_axis=0, tiled=True)
    received_max, received_total = (
        lax.all_to_all(maxima, "ctx", split_axis=0, concat_axis=0, tiled=True),
        lax.all_to_all(totals, "ctx", split_axis=0, concat_axis=0, tiled=True),
    )
    row_peak = jnp.maximum(received_max.max(0), self_max)
    block_scale = jnp.exp(received_max - row_peak[None])
    self_scale = jnp.exp(self_max - row_peak)
    denominator = (block_scale * received_total).sum(0) + self_scale * self_total
    attended = (
        received_numer.astype(jnp.float32) * (block_scale / denominator[None])[..., None]
    ).sum(0)
    attended = attended + self_numer.astype(jnp.float32) * (self_scale / denominator)[..., None]
    logit_part = jnp.dot(
        attended.reshape(positions, channels), unembed.astype(jnp.float32), precision=highest
    )
    logits = lax.psum(logit_part, "tp")
    peak = logits.max(-1, keepdims=True)
    log_total = peak[:, 0] + jnp.log(jnp.exp(logits - peak).sum(-1))
    codes = jnp.where(places == variant_pos[0], allele_ids[0], ref_bases)
    base_ids = jnp.array(BASE_TOKENS, jnp.int32)
    targets = jnp.sum(
        jnp.where(codes[:, None] == jnp.arange(4, dtype=jnp.int32)[None, :], base_ids[None, :], 0),
        -1,
    )
    picked = jnp.sum(
        jnp.where(
            jnp.arange(vocab_size, dtype=jnp.int32)[None, :] == targets[:, None], logits, 0.0
        ),
        -1,
    )
    log_probs = picked - log_total
    variant_scores = jnp.sum(jnp.where(places < cont_lengths[0], log_probs, 0.0))
    return (hyena_row[None], log_probs[None], variant_scores[None])


def solution(mesh):
    placed = (
        P(None, ("ctx", "var"), "tp"),
        P(("ctx", "var"), None, "tp"),
        P(("ctx", "var"), None, "tp"),
        P(None, ("ctx", "var"), None, "tp"),
        P(("ctx", "var"), "tp"),
        P("tp", None),
        P("tp"),
        P("tp", None),
        P(),
        P(("ctx", "var")),
        P(("ctx", "var")),
        P(("ctx", "var")),
    )
    return jax.shard_map(
        on_device,
        mesh=mesh,
        in_specs=placed,
        out_specs=(P(("ctx", "var"), None, "tp"), P(("ctx", "var"), None), P(("ctx", "var"))),
        check_vma=False,
    )
```

profile of v0, /device:TPU:1, one launch (start us, length us, event | category | flops | bytes accessed | tf_op | source)
XLA Modules:
  0.0 692.5 jit_solution(7893740024549596832)
XLA Ops:
  7.2 2.6 copy.120
  10.7 2.9 slice_bitcast_fusion.3
  20.3 263.7 %all-gather = bf16[128,1,2048]{2,1,0:T(2,128)(2,1)S(1)} all-gather(bf16[1,1,2048]{2,1,0:T(2,128)(2,1)S(1)} %bitcast.360), channel_id=1, replica_groups=mesh['ctx'=32,'tp'=4,'var'=4] {'ctx','var'}, dimensions={0}, use_global_device_ids=true | all-gather | bytes 528384 | tf_op jit(solution)/shard_map/all_gather | solution.py:44
  294.3 6.4 fusion.136
  300.7 6.3 fusion.135
  306.9 26.0 %stack.527 = bf16[32,32,2048]{2,1,0:T(8,128)(2,1)} concatenate(bf16[32,1,2048]{2,1,0:T(2,128)(2,1)} %get-tuple-element.127, bf16[32,1,2048]{2,1,0:T(2,128)(2,1)} %get-tuple-element.126, bf16[32,1,2048]{2,1,0:T(2,128)(2,1)} %get-tuple-element.125, bf16[32,1,2048]{2,1,0:T(2,128)(2,1)} %get-tuple-element.124, bf16[32,1,2048]{2,1,0:T(2,128)(2,1)} %get-tuple-element.123, ...), dimensions={1} | concatenate | bytes 8388608 | tf_op jit(solution)/shard_map/stack | solution.py:53
  333.0 6.2 fusion.138
  339.2 6.2 fusion.137
  345.4 26.0 %stack.494 = bf16[32,32,2048]{2,1,0:T(8,128)(2,1)} concatenate(bf16[32,1,2048]{2,1,0:T(2,128)(2,1)} %get-tuple-element.161, bf16[32,1,2048]{2,1,0:T(2,128)(2,1)} %get-tuple-element.160, bf16[32,1,2048]{2,1,0:T(2,128)(2,1)} %get-tuple-element.159, bf16[32,1,2048]{2,1,0:T(2,128)(2,1)} %get-tuple-element.158, bf16[32,1,2048]{2,1,0:T(2,128)(2,1)} %get-tuple-element.157, ...), dimensions={1} | concatenate | bytes 8388608 | tf_op jit(solution)/shard_map/stack | solution.py:53
  372.8 6.2 fusion.139
  379.0 26.3 %stack.461 = bf16[32,32,2048]{2,1,0:T(8,128)(2,1)} concatenate(bf16[32,1,2048]{2,1,0:T(2,128)(2,1)} %get-tuple-element.190, bf16[32,1,2048]{2,1,0:T(2,128)(2,1)} %get-tuple-element.189, bf16[32,1,2048]{2,1,0:T(2,128)(2,1)} %get-tuple-element.188, bf16[32,1,2048]{2,1,0:T(2,128)(2,1)} %get-tuple-element.187, bf16[32,1,2048]{2,1,0:T(2,128)(2,1)} %get-tuple-element.186, ...), dimensions={1} | concatenate | bytes 8388608 | tf_op jit(solution)/shard_map/stack | solution.py:53
  411.1 6.8 fusion.134
  417.9 5.8 copy.154
  426.0 5.8 copy.155
  434.0 5.6 copy.171
  439.6 45.7 %while.14 = (s32[]{:T(128)}, f32[2,512,16]{1,0,2:T(2,128)S(1)}, f32[2,512,16]{1,0,2:T(2,128)}, bf16[2,512,16,128]{3,2,1,0:T(8,128)(2,1)}, bf16[2,512,16,128]{3,2...) while((s32[]{:T(128)}, f32[2,512,16]{1,0,2:T(2,128)S(1)}, ...), condition=%wide.region_8.9_spmd, body=%wide.region_5.8_spmd.sunk | while | flops 1091551232 | bytes 77988040 | solution.py:82
  441.7 4.8 bitcast_reduce_fusion.3
  446.7 4.8 fusion.156
  453.2 5.7 convert_bitcast_fusion.6
  464.4 4.8 bitcast_reduce_fusion.3
  469.4 4.8 fusion.156
  475.9 5.7 convert_bitcast_fusion.6
  489.7 6.1 all-to-all-start.1
  501.8 2.3 all-to-all-done.1
  504.1 6.1 all-to-all-start.2
  510.7 7.6 %all-to-all-done.2 = f32[32,1,512]{2,1,0:T(1,128)S(1)} async-done(((f32[32,1,512]{2,1,0:T(1,128)}), f32[32,1,512]{2,1,0:T(1,128)S(1)}, u32[]{:S(2)}, u32[]{:S(2)}) %all-to-all-start.2) | async-done | bytes 65568 | tf_op jit(solution)/shard_map/all_to_all | solution.py:101
  518.9 4.8 all-to-all-start
  541.8 3.8 multiply_reduce_fusion.4
  545.6 3.0 multiply_reduce_fusion.1
  557.8 66.8 %all-to-all-done = bf16[32,32,16,128]{3,2,1,0:T(8,128)(2,1)} async-done(((bf16[32,32,16,128]{3,2,1,0:T(8,128)(2,1)}), bf16[32,32,16,128]{3,2,1,0:T(8,128)(2,1)}, u32[]{:S(2)}, u32[]{:S(2)}) %all-to-all-start) | async-done | bytes 4194336 | tf_op jit(solution)/shard_map/all_to_all | solution.py:98
  624.7 4.5 multiply_reduce_fusion
  631.5 50.9 %all-reduce.2.cloned.1.call-done = f32[32,512]{1,0:T(8,128)} async-done(((f32[32,512]{1,0:T(8,128)}), f32[32,512]{1,0:T(8,128)}) %all-reduce.2.cloned.1.call-update) | async-done | bytes 65552 | tf_op jit(solution)/shard_map/psum | solution.py:114
  (160 shorter events, 86.2 us)
Async XLA Ops:
  7.2 622.4 %copy-start = (bf16[2048,512]{1,0:T(8,128)(2,1)S(1)}, bf16[2048,512]{1,0:T(8,128)(2,1)}, u32[]{:S(2)}) copy-start(bf16[2048,512]{1,0:T(8,128)(2,1)} %param.22) | copy-start | bytes 6291460
  7.2 3.5 copy-start.6
  7.2 403.9 %all-gather.6.cloned.1.call-start = ((), (), s32[]{:S(2)}) async-start(), calls=%async_computation.4 | async-start | bytes 2621440 | tf_op jit(solution)/shard_map/all_gather | solution.py:65
  9.9 424.1 %all-gather.4.cloned.1.call-start = ((), (), s32[]{:S(2)}) async-start(), calls=%async_computation.3 | async-start | bytes 4325376 | tf_op jit(solution)/shard_map/all_gather | solution.py:68
  10.7 9.6 %copy-start.24 = (bf16[1,2048]{1,0:T(2,128)(2,1)S(1)}, bf16[1,2048]{1,0:T(2,128)(2,1)}, u32[]{:S(2)}) copy-start(bf16[1,2048]{1,0:T(2,128)(2,1)} %param.19) | copy-start | bytes 12292
  13.6 273.7 %copy-start.18 = (bf16[1,32,2048]{2,1,0:T(8,128)(2,1)S(1)}, bf16[1,32,2048]{2,1,0:T(8,128)(2,1)}, u32[]{:S(2)}) copy-start(bf16[1,32,2048]{2,1,0:T(8,128)(2,1)} %param.16) | copy-start | bytes 393220
  379.0 26.3 %copy-start.1 = (bf16[128,1,2048]{2,0,1:T(8,128)(2,1)S(1)}, bf16[128,1,2048]{2,0,1:T(8,128)(2,1)}, u32[]{:S(2)}) copy-start(bf16[128,1,2048]{2,0,1:T(8,128)(2,1)} %copy.212) | copy-start | bytes 1572868
  405.3 5.6 copy-start.20
  405.3 5.6 copy-start.21
  411.1 112.8 %copy-start.16 = (f32[32,16,32]{0,2,1:T(8,128)}, f32[32,16,32]{0,2,1:T(8,128)S(1)}, u32[]{:S(2)}) copy-start(f32[32,16,32]{0,2,1:T(8,128)S(1)} %get-tuple-element.194) | copy-start | bytes 196612
  434.0 5.6 copy-start.22
  439.6 70.5 %copy-start.25 = (s32[32]{0:T(128)S(1)}, s32[32]{0:T(128)}, u32[]{:S(2)}) copy-start(s32[32]{0:T(128)} %param.23) | copy-start | bytes 388
  453.2 5.7 copy-start.7
  475.9 5.7 copy-start.7
  489.7 14.4 %all-to-all-start.1 = ((f32[32,1,512]{2,1,0:T(1,128)}), f32[32,1,512]{2,1,0:T(1,128)S(1)}, u32[]{:S(2)}, u32[]{:S(2)}) async-start(f32[32,1,512]{2,1,0:T(1,128)} %reshape.433), calls=%async_computation.1 | async-start | bytes 131072 | tf_op jit(solution)/shard_map/all_to_all | solution.py:100
  504.1 14.2 %all-to-all-start.2 = ((f32[32,1,512]{2,1,0:T(1,128)}), f32[32,1,512]{2,1,0:T(1,128)S(1)}, u32[]{:S(2)}, u32[]{:S(2)}) async-start(f32[32,1,512]{2,1,0:T(1,128)} %reshape.435), calls=%async_computation.2 | async-start | bytes 131072 | tf_op jit(solution)/shard_map/all_to_all | solution.py:101
  518.9 105.7 %all-to-all-start = ((bf16[32,32,16,128]{3,2,1,0:T(8,128)(2,1)}), bf16[32,32,16,128]{3,2,1,0:T(8,128)(2,1)}, u32[]{:S(2)}, u32[]{:S(2)}) async-start(bf16[32,32,16,128]{3,2,1,0:T(8,128)(2,1)} %bitcast.348), calls=%async_computation | async-start | bytes 8388608 | tf_op jit(solution)/shard_map/all_to_all | solution.py:98
  523.8 158.6 %all-reduce.2.cloned.1.call-start = ((), (), s32[]{:S(2)}) async-start(), calls=%async_computation.5 | async-start | bytes 131072 | tf_op jit(solution)/shard_map/psum | solution.py:114
  532.2 7.6 %copy-start.5 = (bf16[32,32,2048]{2,1,0:T(8,128)(2,1)S(1)}, bf16[32,32,2048]{2,1,0:T(8,128)(2,1)}, u32[]{:S(2)}) copy-start(bf16[32,32,2048]{2,1,0:T(8,128)(2,1)} %stack.461) | copy-start | bytes 12582916
  532.2 7.6 %copy-start.12 = (f32[32,2048]{1,0:T(8,128)S(1)}, f32[32,2048]{1,0:T(8,128)}, u32[]{:S(2)}) copy-start(f32[32,2048]{1,0:T(8,128)} %copy.117) | copy-start | bytes 786436
  536.3 4.8 copy-start.15
  539.8 5.8 copy-start.3
  539.8 5.8 copy-start.4
  539.8 5.8 copy-start.10
  539.8 5.8 copy-start.11
  545.6 3.0 copy-start.9
  545.6 3.0 copy-start.23
  557.8 73.5 %copy-start.26 = (s32[32]{0:T(128)S(1)}, s32[32]{0:T(128)}, u32[]{:S(2)}) copy-start(s32[32]{0:T(128)} %compare_select_fusion.1) | copy-start | bytes 388
  557.8 73.5 %copy-start.27 = (s32[4]{0:T(128)S(1)}, s32[4]{0:T(128)}, u32[]{:S(2)}) copy-start(s32[4]{0:T(128)} %constant.31.clone) | copy-start | bytes 52
  624.7 4.5 copy-start.13
  624.7 4.5 copy-start.14
  624.7 4.5 copy-start.17
  (5 other events, 8.6 us)
Sparse Core Ops, SparseCore 0:
  10.1 58.2 all-gather.5
  70.6 73.5 all-gather.3
  631.5 50.8 all-reduce.1
where the time goes:
time: 705 us; the launch traced here: 692 us
  blocking collectives  264 us (37%)
  local copies, waits for them, and re-layouts  187 us (27%)
  waiting for transfers between devices  128 us (18%)
  other arithmetic  55.7 us (8%)
  matrix products  23.4 us (3%)
  starting transfers between devices  17.1 us (2%)
  between operations  16.6 us (2%)
    all_gather x1, blocking collectives, on_device(): past_rows = lax.all_gather(hyena_state, ('ctx', 'var'), axis=0, tiled=True)  264 us
    another operation x4, local copies, waits for them, and re-layouts, on_device(): jnp.stack([lax.slice_in_dim(sequence, filter_len - offset, filter_len - o...  79.1 us
    all_to_all x1, waiting for transfers between devices, on_device(): lax.all_to_all(numerators, 'ctx', split_axis=0, concat_axis=0, tiled=True)  66.8 us
    psum x1, waiting for transfers between devices, on_device(): logits = lax.psum(logit_part, 'tp')  50.9 us
    slice x6, local copies, waits for them, and re-layouts, on_device(): lax.slice_in_dim(sequence, filter_len - offset, filter_len - offset + pos...  32.7 us
    unnamed x63, local copies, waits for them, and re-layouts  29.8 us
    unnamed x33, other arithmetic  23.4 us
  transfers between devices with their start and end apart: 6, of which 4 were waited for; matrix products, arithmetic and copies ran while one was open for 29% of the time, Pallas kernels for 0%

commit v1 on v0

v1 whole, which is shorter than its diff:
```python
import functools
import math

import jax
import jax.numpy as jnp
from jax import lax
from jax.experimental import pallas as pl
from jax.experimental.pallas import tpu as pltpu
from jax.sharding import PartitionSpec as P

HEAD_DIM = 128
BASE_TOKENS = (65, 67, 71, 84)
EXP_SCALE = HEAD_DIM ** (-0.5) * math.log2(math.e)
LOWEST = -3.0e38
BF16 = jnp.bfloat16
F32 = jnp.float32


def spread_kernel(
    n,
    tp_count,
    kv_ref,
    q_ref,
    ck_ref,
    hy_ref,
    state_ref,
    filt_ref,
    skip_ref,
    unembed_ref,
    bases_ref,
    pos_ref,
    allele_ref,
    length_ref,
    hyena_ref,
    log_probs_ref,
    score_ref,
    q_own,
    kv_own,
    state_src,
    state_all,
    state_rows,
    gather_r,
    gather_l,
    gather_far,
    part_out_r,
    part_out_l,
    part_far,
    stat_out_r,
    stat_out_l,
    stat_far,
    part_in_r,
    part_in_l,
    stat_in_r,
    stat_in_l,
    values_t,
    merged,
    merged_stat,
    back,
    back_stat,
    state_part,
    state_parts,
    stat_square,
    logit_parts,
    targets,
    padded,
    mixed,
    taps_own,
    q_v,
    ck_v,
    hy_v,
    filt_v,
    unembed_v,
    local_sem,
    spread_send,
    spread_recv,
    gather_send_r,
    gather_recv_r,
    gather_send_l,
    gather_recv_l,
    part_send,
    part_recv_r,
    part_recv_l,
    stat_send,
    stat_recv_r,
    stat_recv_l,
    back_send,
    back_recv,
    tp_send,
    tp_recv,
):
    half = n // 2
    heads = 2 * n
    positions = q_v.shape[0]
    rows = heads * positions
    taps = filt_v.shape[1]
    channels = heads * HEAD_DIM
    vocab = unembed_v.shape[1]

    ctx = lax.axis_index("ctx")
    var = lax.axis_index("var")
    tp = lax.axis_index("tp")
    z = lax.div(ctx, 4)
    core = lax.rem(ctx, 2)
    y = var * 2 + lax.div(lax.rem(ctx, 4), 2)
    ring = (1 - core) * z + core * y
    other = (1 - core) * y + core * z
    head = (1 - core) * y + core * (n + z)

    def device(z_to, y_to, core_to):
        return {"ctx": z_to * 4 + lax.rem(y_to, 2) * 2 + core_to, "var": lax.div(y_to, 2)}

    def ring_device(offset):
        return device(
            lax.rem(z + offset * (1 - core), n), lax.rem(y + offset * core, n), core
        )

    def remote(src, dst, send_sem, recv_sem, device_id):
        return pltpu.make_async_remote_copy(
            src_ref=src,
            dst_ref=dst,
            send_sem=send_sem,
            recv_sem=recv_sem,
            device_id=device_id,
            device_id_type=pl.DeviceIdType.MESH,
        )

    def wait_for(ref, sem):
        pltpu.make_async_copy(ref, ref, sem).wait()

    def lanes_of(h):
        return pl.ds(pl.multiple_of(h * HEAD_DIM, HEAD_DIM), HEAD_DIM)

    loads = [
        pltpu.make_async_copy(hy_ref.at[:, 0], hy_v, local_sem.at[0]),
        pltpu.make_async_copy(filt_ref, filt_v, local_sem.at[1]),
        pltpu.make_async_copy(q_ref.at[0], q_v, local_sem.at[2]),
        pltpu.make_async_copy(ck_ref.at[0], ck_v, local_sem.at[3]),
        pltpu.make_async_copy(unembed_ref, unembed_v, local_sem.at[4]),
    ]
    for load in loads:
        load.start()

    cut = rows // 2
    part_in_r[half - 1, :, cut:] = jnp.zeros((HEAD_DIM, cut), BF16)
    part_in_l[half - 1, :, :cut] = jnp.zeros((HEAD_DIM, cut), BF16)
    stat_in_r[half - 1, 0:1, cut:] = jnp.full((1, cut), LOWEST, F32)
    stat_in_l[half - 1, 0:1, :cut] = jnp.full((1, cut), LOWEST, F32)
    stat_in_r[half - 1, 1:2, cut:] = jnp.zeros((1, cut), F32)
    stat_in_l[half - 1, 1:2, :cut] = jnp.zeros((1, cut), F32)
    for h in range(heads):
        state_src[h] = state_ref[:, h * HEAD_DIM : (h + 1) * HEAD_DIM].astype(F32)

    barrier = pltpu.get_barrier_semaphore()

    def greet(device_id):
        pl.semaphore_signal(
            barrier, inc=1, device_id=device_id, device_id_type=pl.DeviceIdType.MESH
        )

    def greet_offset(k, carry):
        for c_to in range(2):
            greet(device(z, lax.rem(y + k, n), c_to))
            greet(device(lax.rem(z + k, n), y, c_to))
        return carry

    lax.fori_loop(1, n, greet_offset, 0)
    greet(device(z, y, 1 - core))
    for k in range(1, tp_count):
        greet({"tp": lax.rem(tp + k, tp_count)})
    pl.semaphore_wait(barrier, 4 * (n - 1) + 1 + tp_count - 1)

    slot_y = 2 * y + core
    slot_z = 2 * z + core
    slot_self = 2 * other + core
    slot_sibling = 2 * ring + core
    head_sibling = (1 - core) * (n + z) + core * y
    sibling = device(z, y, 1 - core)

    def q_copy(h, slot, device_id):
        return remote(
            q_ref.at[0, :, lanes_of(h)],
            q_own.at[slot],
            spread_send.at[0],
            spread_recv.at[0],
            device_id,
        )

    def state_copy(h, ring_to, slot, device_id):
        return remote(
            state_src.at[h],
            state_all.at[ring_to, slot],
            spread_send.at[1],
            spread_recv.at[1],
            device_id,
        )

    def kv_copy(h, slot, device_id):
        return remote(
            kv_ref.at[:, :, lanes_of(h)],
            kv_own.at[slot],
            spread_send.at[2],
            spread_recv.at[2],
            device_id,
        )

    def send_q(k, carry):
        y_to = lax.rem(y + k, n)
        z_to = lax.rem(z + k, n)
        q_copy(y_to, slot_y, device(z, y_to, 0)).start()
        q_copy(n + z_to, slot_z, device(z_to, y, 1)).start()
        state_copy(y_to, z, slot_y, device(z, y_to, 0)).start()
        state_copy(n + z_to, y, slot_z, device(z_to, y, 1)).start()
        return carry

    def send_kv(k, carry):
        y_to = lax.rem(y + k, n)
        z_to = lax.rem(z + k, n)
        kv_copy(y_to, slot_y, device(z, y_to, 0)).start()
        kv_copy(n + z_to, slot_z, device(z_to, y, 1)).start()
        return carry

    self_q = pltpu.make_async_copy(
        q_ref.at[0, :, lanes_of(head)], q_own.at[slot_self], local_sem.at[5]
    )
    self_kv = pltpu.make_async_copy(
        kv_ref.at[:, :, lanes_of(head)], kv_own.at[slot_self], local_sem.at[6]
    )
    self_state = pltpu.make_async_copy(
        state_src.at[head], state_all.at[ring, slot_self], local_sem.at[7]
    )
    lax.fori_loop(1, n, send_q, 0)
    q_copy(head_sibling, slot_sibling, sibling).start()
    state_copy(head_sibling, other, slot_sibling, sibling).start()
    self_q.start()
    self_state.start()
    lax.fori_loop(1, n, send_kv, 0)
    kv_copy(head_sibling, slot_sibling, sibling).start()
    self_kv.start()

    loads[0].wait()
    product = (hy_v[1].astype(F32) * hy_v[2].astype(F32)).astype(BF16).astype(F32)
    padded[0:positions, :] = jnp.zeros((positions, channels), F32)
    padded[positions:, :] = product
    mixed[...] = skip_ref[...] * product
    row_index = lax.broadcasted_iota(jnp.int32, (positions, vocab), 0)
    codes = jnp.zeros((positions, vocab), jnp.int32)
    for t in range(positions):
        codes = jnp.where(row_index == t, bases_ref[t], codes)
    codes = jnp.where(row_index == pos_ref[0], allele_ref[0], codes)
    wanted = jnp.zeros((positions, vocab), jnp.int32)
    for code, token in enumerate(BASE_TOKENS):
        wanted = jnp.where(codes == code, token, wanted)
    targets[...] = wanted

    right = ring_device(1)
    left = ring_device(n - 1)
    part = heads // 2

    def gather_right(d, src):
        if d < half:
            return remote(
                src, gather_r.at[d - 1], gather_send_r.at[d - 1], gather_recv_r.at[d - 1], right
            )
        return remote(
            src.at[0:part],
            gather_far.at[0:part],
            gather_send_r.at[d - 1],
            gather_recv_r.at[d - 1],
            right,
        )

    def gather_left(d, src):
        if d < half:
            return remote(
                src, gather_l.at[d - 1], gather_send_l.at[d - 1], gather_recv_l.at[d - 1], left
            )
        return remote(
            src.at[part:heads],
            gather_far.at[part:heads],
            gather_send_l.at[d - 1],
            gather_recv_l.at[d - 1],
            left,
        )

    gathers = []

    def pass_on(d):
        for copy in (
            gather_right(d, q_own if d == 1 else gather_r.at[d - 2]),
            gather_left(d, q_own if d == 1 else gather_l.at[d - 2]),
        ):
            copy.start()
            gathers.append(copy)

    wait_for(q_own.at[0 : heads - 1], spread_recv.at[0])
    self_q.wait()
    pass_on(1)

    wait_for(state_all.at[0, 0 : heads - 1], spread_recv.at[1])
    self_state.wait()

    def send_state(k, carry):
        remote(
            state_all.at[ring],
            state_all.at[ring],
            spread_send.at[3],
            spread_recv.at[3],
            ring_device(k),
        ).start()
        return carry

    lax.fori_loop(1, n, send_state, 0)

    loads[1].wait()

    def own_taps(h, carry):
        lanes = lanes_of(h)
        coeffs = jnp.transpose(filt_v[lanes, :])
        total = mixed[:, lanes]
        for j in range(1, positions):
            total = total + padded[positions - j : 2 * positions - j, lanes] * coeffs[j - 1 : j, :]
        mixed[:, lanes] = total
        return carry

    lax.fori_loop(0, part, own_taps, 0)
    if half > 1:
        for copy in gathers[-2:]:
            copy.wait_recv()
        pass_on(2)
    lax.fori_loop(part, heads, own_taps, 0)
    if half > 2:
        for copy in gathers[-2:]:
            copy.wait_recv()
        pass_on(3)

    taps_own[...] = jnp.transpose(filt_v[lanes_of(head), :])
    state_rows[taps:, :] = jnp.zeros((positions, HEAD_DIM), F32)
    wait_for(state_all.at[0 : n - 1], spread_recv.at[3])

    def place_row(index, carry):
        at = lax.div(index, heads)
        slot = lax.rem(index, heads)
        spot = lax.div(slot, 2)
        z_of = (1 - core) * at + core * spot
        y_of = (1 - core) * spot + core * at
        row = (z_of * 4 + lax.rem(y_of, 2) * 2 + lax.rem(slot, 2)) * half + lax.div(y_of, 2)
        state_rows[pl.ds(row, 1), :] = state_all[at, slot]
        return carry

    lax.fori_loop(0, n * heads, place_row, 0)

    def state_taps(step, total):
        base = pl.multiple_of(step * 8, 8)
        for b in range(8):
            total = total + (
                state_rows[pl.ds(base + b, positions), :]
                * taps_own[pl.ds(taps - 1 - b - base, 1), :]
            )
        return total

    state_part[...] = lax.fori_loop(
        0, taps // 8, state_taps, jnp.zeros((positions, HEAD_DIM), F32)
    ).astype(BF16)

    def back_device(k, c_to):
        spot = lax.rem(other + k, n)
        return (
            2 * spot + c_to,
            device((1 - core) * z + core * spot, (1 - core) * spot + core * y, c_to),
        )

    def state_back(device_id):
        return remote(
            state_part, state_parts.at[head], back_send.at[0], back_recv.at[0], device_id
        )

    def send_state_back(k, carry):
        for c_to in range(2):
            state_back(back_device(k, c_to)[1]).start()
        return carry

    lax.fori_loop(1, n, send_state_back, 0)
    state_back(sibling).start()
    state_parts[head] = state_part[...]

    if half > 3:
        for d in range(4, half + 1):
            for copy in gathers[-2:]:
                copy.wait_recv()
            pass_on(d)

    wait_for(kv_own.at[0 : heads - 1], spread_recv.at[2])
    self_kv.wait()
    context = heads * kv_own.shape[2]
    values_t[...] = jnp.transpose(kv_own[:, 1].reshape(context, HEAD_DIM))

    def attend(chunk):
        keys = kv_own[:, 0].reshape(context, HEAD_DIM)
        numer, peak, total = [], [], []
        width = min(256, rows)
        for first in range(0, rows, width):
            block = chunk[first : first + width]
            scores = lax.dot_general(
                keys, block, (((1,), (1,)), ((), ())), preferred_element_type=F32
            )
            top = jnp.max(scores, 0, keepdims=True)
            weights = jnp.exp2((scores - top) * EXP_SCALE)
            peak.append(top)
            total.append(jnp.sum(weights, 0, keepdims=True))
            numer.append(
                jnp.dot(values_t[...], weights.astype(BF16), preferred_element_type=F32)
            )
        return (
            jnp.concatenate(numer, 1),
            jnp.concatenate(peak, 1),
            jnp.concatenate(total, 1),
        )

    def merge(a, b):
        peak = jnp.maximum(a[1], b[1])
        scale_a = jnp.exp2((a[1] - peak) * EXP_SCALE)
        scale_b = jnp.exp2((b[1] - peak) * EXP_SCALE)
        return (a[0] * scale_a + b[0] * scale_b, peak, a[2] * scale_a + b[2] * scale_b)

    def arrived(part_in, stat_in, s):
        return (part_in[s].astype(F32), stat_in[s, 0:1, :], stat_in[s, 1:2, :])

    for copy in gathers[-2:]:
        copy.wait_recv()
    far = attend(gather_far[...].reshape(rows, HEAD_DIM))
    part_far[...] = far[0].astype(BF16)
    stat_far[0:1, :] = far[1]
    stat_far[1:2, :] = far[2]
    far_copies = []
    for side, part_in, stat_in, part_recv, stat_recv, device_id in (
        (0, part_in_r, stat_in_r, part_recv_r, stat_recv_r, right),
        (1, part_in_l, stat_in_l, part_recv_l, stat_recv_l, left),
    ):
        span = pl.ds(side * cut, cut)
        far_copies.append(
            remote(
                part_far.at[:, span],
                part_in.at[half - 1, :, span],
                part_send.at[side, half - 1],
                part_recv.at[half - 1],
                device_id,
            )
        )
        far_copies.append(
            remote(
                stat_far.at[:, span],
                stat_in.at[half - 1, :, span],
                stat_send.at[side, half - 1],
                stat_recv.at[half - 1],
                device_id,
            )
        )
    for copy in far_copies:
        copy.start()

    wait_for(state_parts.at[0 : heads - 1], back_recv.at[0])
    for h in range(heads):
        lanes = slice(h * HEAD_DIM, (h + 1) * HEAD_DIM)
        hyena_ref[0, :, lanes] = (
            hy_v[0, :, lanes].astype(F32) * (mixed[:, lanes] + state_parts[h].astype(F32))
        ).astype(BF16)
    loads[2].wait()
    loads[3].wait()
    group = HEAD_DIM // positions
    own = []
    row_at = lax.broadcasted_iota(jnp.int32, (HEAD_DIM, HEAD_DIM), 0)
    col_at = lax.broadcasted_iota(jnp.int32, (HEAD_DIM, HEAD_DIM), 1)
    seen = (lax.div(row_at, positions) == lax.div(col_at, positions)) & (col_at <= row_at)

    def stacked(ref, g):
        return jnp.concatenate(
            [ref[:, h * HEAD_DIM : (h + 1) * HEAD_DIM] for h in range(g * group, (g + 1) * group)],
            0,
        )

    for g in range(heads // group):
        scores = lax.dot_general(
            stacked(q_v, g), stacked(ck_v, g), (((1,), (1,)), ((), ())), preferred_element_type=F32
        )
        scores = jnp.where(seen, scores, LOWEST)
        top = jnp.max(scores, 1, keepdims=True)
        weights = jnp.where(seen, jnp.exp2((scores - top) * EXP_SCALE), 0.0)
        total = jnp.sum(weights, 1, keepdims=True)
        numer = jnp.dot(
            weights.astype(BF16), stacked(hyena_ref.at[0], g), preferred_element_type=F32
        )
        own.append((numer, top, total))

    def part_copy(s, side):
        part_out, part_in, part_recv, device_id = (
            (part_out_r, part_in_r, part_recv_r, right),
            (part_out_l, part_in_l, part_recv_l, left),
        )[side]
        return remote(
            part_out.at[s],
            part_in.at[s - 1],
            part_send.at[side, s - 1],
            part_recv.at[s - 1],
            device_id,
        )

    def stat_copy(s, side):
        stat_out, stat_in, stat_recv, device_id = (
            (stat_out_r, stat_in_r, stat_recv_r, right),
            (stat_out_l, stat_in_l, stat_recv_l, left),
        )[side]
        return remote(
            stat_out.at[s],
            stat_in.at[s - 1],
            stat_send.at[side, s - 1],
            stat_recv.at[s - 1],
            device_id,
        )

    def wait_part(s, side, span):
        part_in, part_recv, stat_in, stat_recv = (
            (part_in_r, part_recv_r, stat_in_r, stat_recv_r),
            (part_in_l, part_recv_l, stat_in_l, stat_recv_l),
        )[side]
        wait_for(part_in.at[s, :, span], part_recv.at[s])
        wait_for(stat_in.at[s, :, span], stat_recv.at[s])

    def reduce_step(s, span_r, span_l):
        for side, gathered, part_in, stat_in, part_out, stat_out, span in (
            (0, gather_l, part_in_r, stat_in_r, part_out_r, stat_out_r, span_r),
            (1, gather_r, part_in_l, stat_in_l, part_out_l, stat_out_l, span_l),
        ):
            mine = attend(gathered[s - 1].reshape(rows, HEAD_DIM))
            wait_part(s, side, span)
            numer, peak, total = merge(mine, arrived(part_in, stat_in, s))
            part_out[s] = numer.astype(BF16)
            stat_out[s, 0:1, :] = peak
            stat_out[s, 1:2, :] = total
            part_copy(s, side).start()
            stat_copy(s, side).start()

    whole = pl.ds(0, rows)
    first_r, first_l = pl.ds(0, cut), pl.ds(cut, cut)
    if half > 1:
        reduce_step(half - 1, first_r, first_l)

    def reduce_more(index, carry):
        reduce_step(half - 2 - index, whole, whole)
        return carry

    if half > 2:
        lax.fori_loop(0, half - 2, reduce_more, 0)

    mine = attend(q_own[...].reshape(rows, HEAD_DIM))
    wait_part(0, 0, whole if half > 1 else first_r)
    mine = merge(mine, arrived(part_in_r, stat_in_r, 0))
    wait_part(0, 1, whole if half > 1 else first_l)
    numer, peak, total = merge(mine, arrived(part_in_l, stat_in_l, 0))
    merged[...] = jnp.transpose(numer).astype(BF16).reshape(merged.shape)
    for b in range(rows // HEAD_DIM):
        merged_stat[b, 0:1, :] = peak[:, b * HEAD_DIM : (b + 1) * HEAD_DIM]
        merged_stat[b, 1:2, :] = total[:, b * HEAD_DIM : (b + 1) * HEAD_DIM]

    def back_copy(slot, device_id):
        return remote(
            merged.at[slot], back.at[head], back_send.at[1], back_recv.at[1], device_id
        )

    def back_stat_copy(slot, device_id):
        return remote(
            merged_stat.at[lax.div(slot, group)],
            back_stat.at[head],
            back_send.at[2],
            back_recv.at[2],
            device_id,
        )

    def send_back(k, carry):
        for c_to in range(2):
            slot, device_id = back_device(k, c_to)
            back_copy(slot, device_id).start()
            back_stat_copy(slot, device_id).start()
        return carry

    lax.fori_loop(1, n, send_back, 0)
    slot_other = 2 * other + 1 - core
    back_copy(slot_other, sibling).start()
    back_stat_copy(slot_other, sibling).start()
    back[head] = merged[slot_self]
    back_stat[head] = merged_stat[lax.div(slot_self, group)]

    loads[4].wait()
    stat_square[...] = jnp.zeros_like(stat_square)
    wait_for(back_stat.at[0 : heads - 1], back_recv.at[2])
    for first, slot in ((0, slot_y), (n, slot_z)):
        shift = lax.rem(HEAD_DIM - lax.rem(slot, group) * positions, HEAD_DIM)
        for kind in range(2):
            stat_square[kind * heads + first : kind * heads + first + n, :] = pltpu.roll(
                back_stat[first : first + n, kind, :], shift, 1
            )
    columns = jnp.transpose(stat_square[...])
    wait_for(back.at[0 : heads - 1], back_recv.at[1])
    pieces = []
    for g in range(heads // group):
        chosen = range(g * group, (g + 1) * group)
        peak = jnp.concatenate([columns[0:positions, h : h + 1] for h in chosen], 0)
        total = jnp.concatenate(
            [columns[0:positions, heads + h : heads + h + 1] for h in chosen], 0
        )
        numer = back[g * group : (g + 1) * group].reshape(HEAD_DIM, HEAD_DIM).astype(F32)
        numer, _, total = merge((numer, peak, total), own[g])
        attended = numer / total
        pieces += [attended[i * positions : (i + 1) * positions] for i in range(group)]
    attended = jnp.concatenate(pieces, 1)
    high = attended.astype(BF16)
    low = (attended - high.astype(F32)).astype(BF16)
    both = jnp.dot(
        jnp.concatenate([high, low], 0), unembed_v[...], preferred_element_type=F32
    )
    logit_parts[tp] = both[0:positions] + both[positions:]

    tp_copies = [
        remote(
            logit_parts.at[tp],
            logit_parts.at[tp],
            tp_send,
            tp_recv,
            {"tp": lax.rem(tp + k, tp_count)},
        )
        for k in range(1, tp_count)
    ]
    for copy in tp_copies:
        copy.start()
    if tp_count > 1:
        wait_for(logit_parts.at[0 : tp_count - 1], tp_recv)
    logits = logit_parts[0]
    for k in range(1, tp_count):
        logits = logits + logit_parts[k]
    top = jnp.max(logits, 1, keepdims=True)
    log_total = top + jnp.log(jnp.sum(jnp.exp(logits - top), 1, keepdims=True))
    vocab_at = lax.broadcasted_iota(jnp.int32, (positions, vocab), 1)
    picked = jnp.sum(jnp.where(vocab_at == targets[...], logits, 0.0), 1, keepdims=True)
    log_probs = picked - log_total
    place = lax.broadcasted_iota(jnp.int32, (positions, positions), 0)
    lane = lax.broadcasted_iota(jnp.int32, (positions, positions), 1)
    log_row = jnp.sum(jnp.where(place == lane, log_probs, 0.0), 0, keepdims=True)
    log_probs_ref[...] = log_row
    lane_row = lax.broadcasted_iota(jnp.int32, (1, positions), 1)
    score_ref[...] = jnp.sum(
        jnp.where(lane_row < length_ref[0], log_row, 0.0), 1, keepdims=True
    )

    wait_for(q_own.at[0 : heads - 1], spread_send.at[0])
    wait_for(state_all.at[0, 0 : heads - 1], spread_send.at[1])
    wait_for(kv_own.at[0 : heads - 1], spread_send.at[2])
    wait_for(state_all.at[0 : n - 1], spread_send.at[3])
    for copy in gathers + far_copies:
        copy.wait_send()
    for s in range(1, half):
        for side in range(2):
            part_copy(s, side).wait_send()
            stat_copy(s, side).wait_send()
    wait_for(state_parts.at[0 : heads - 1], back_send.at[0])
    wait_for(back.at[0 : heads - 1], back_send.at[1])
    wait_for(back_stat.at[0 : heads - 1], back_send.at[2])
    if tp_count > 1:
        wait_for(logit_parts.at[0 : tp_count - 1], tp_send)


def on_device(
    n,
    tp_count,
    context_kv,
    queries,
    cont_keys,
    hyena_inputs,
    hyena_state,
    hyena_filter,
    filter_skip,
    unembed,
    ref_bases,
    variant_pos,
    allele_ids,
    cont_lengths,
):
    positions, channels = queries.shape[1:]
    block = context_kv.shape[1]
    taps = hyena_filter.shape[1]
    vocab = unembed.shape[1]
    heads = channels // HEAD_DIM
    half = n // 2
    rows = heads * positions
    steps = max(1, half - 1)
    vmem = pltpu.VMEM
    dma = pltpu.SemaphoreType.DMA
    scratch = [
        vmem((heads, positions, HEAD_DIM), BF16),
        vmem((heads, 2, block, HEAD_DIM), BF16),
        vmem((heads, 1, HEAD_DIM), F32),
        vmem((n, heads, 1, HEAD_DIM), F32),
        vmem((taps + positions, HEAD_DIM), F32),
        vmem((steps, heads, positions, HEAD_DIM), BF16),
        vmem((steps, heads, positions, HEAD_DIM), BF16),
        vmem((heads, positions, HEAD_DIM), BF16),
        vmem((half, HEAD_DIM, rows), BF16),
        vmem((half, HEAD_DIM, rows), BF16),
        vmem((HEAD_DIM, rows), BF16),
        vmem((half, 2, rows), F32),
        vmem((half, 2, rows), F32),
        vmem((2, rows), F32),
        vmem((half, HEAD_DIM, rows), BF16),
        vmem((half, HEAD_DIM, rows), BF16),
        vmem((half, 2, rows), F32),
        vmem((half, 2, rows), F32),
        vmem((HEAD_DIM, heads * block), BF16),
        vmem((heads, positions, HEAD_DIM), BF16),
        vmem((rows // HEAD_DIM, 2, HEAD_DIM), F32),
        vmem((heads, positions, HEAD_DIM), BF16),
        vmem((heads, 2, HEAD_DIM), F32),
        vmem((positions, HEAD_DIM), BF16),
        vmem((heads, positions, HEAD_DIM), BF16),
        vmem((HEAD_DIM, HEAD_DIM), F32),
        vmem((tp_count, positions, vocab), F32),
        vmem((positions, vocab), jnp.int32),
        vmem((2 * positions, channels), F32),
        vmem((positions, channels), F32),
        vmem((taps, HEAD_DIM), F32),
        vmem((positions, channels), BF16),
        vmem((positions, channels), BF16),
        vmem((3, positions, channels), BF16),
        vmem((channels, taps), F32),
        vmem((channels, vocab), BF16),
        dma((8,)),
        dma((4,)),
        dma((4,)),
        dma((half,)),
        dma((half,)),
        dma((half,)),
        dma((half,)),
        dma((2, half)),
        dma((half,)),
        dma((half,)),
        dma((2, half)),
        dma((half,)),
        dma((half,)),
        dma((3,)),
        dma((3,)),
        dma,
        dma,
    ]
    hbm = pl.BlockSpec(memory_space=pl.ANY)
    in_vmem = pl.BlockSpec(memory_space=pltpu.VMEM)
    in_smem = pl.BlockSpec(memory_space=pltpu.SMEM)
    hyena_out, log_probs, score = pl.pallas_call(
        functools.partial(spread_kernel, n, tp_count),
        out_shape=(
            jax.ShapeDtypeStruct((1, positions, channels), BF16),
            jax.ShapeDtypeStruct((1, positions), F32),
            jax.ShapeDtypeStruct((1, 1), F32),
        ),
        in_specs=[hbm] * 4 + [in_vmem, hbm, in_vmem, hbm] + [in_smem] * 4,
        out_specs=(in_vmem, in_vmem, in_vmem),
        scratch_shapes=scratch,
        compiler_params=pltpu.CompilerParams(
            collective_id=0, has_side_effects=True, vmem_limit_bytes=48 * 1024 * 1024
        ),
    )(
        context_kv,
        queries,
        cont_keys,
        hyena_inputs,
        hyena_state,
        hyena_filter,
        filter_skip.reshape(1, channels),
        unembed,
        ref_bases,
        variant_pos,
        allele_ids,
        cont_lengths,
    )
    return hyena_out, log_probs, score.reshape(1)


def solution(mesh):
    n = mesh.shape["ctx"] // 4
    placed = (
        P(None, ("ctx", "var"), "tp"),
        P(("ctx", "var"), None, "tp"),
        P(("ctx", "var"), None, "tp"),
        P(None, ("ctx", "var"), None, "tp"),
        P(("ctx", "var"), "tp"),
        P("tp", None),
        P("tp"),
        P("tp", None),
        P(),
        P(("ctx", "var")),
        P(("ctx", "var")),
        P(("ctx", "var")),
    )
    return jax.shard_map(
        functools.partial(on_device, n, mesh.shape["tp"]),
        mesh=mesh,
        in_specs=placed,
        out_specs=(P(("ctx", "var"), None, "tp"), P(("ctx", "var"), None), P(("ctx", "var"))),
        check_vma=False,
    )
```

time: 705 us -> 89.1 us (0.13); the launches traced: 692 us -> 88.7 us
  blocking collectives: 264 us -> 0 us
  local copies, waits for them, and re-layouts: 187 us -> 9.87 us
  waiting for transfers between devices: 128 us -> 0 us
  Pallas kernels: 0 us -> 74.5 us
  other arithmetic: 55.7 us -> 0 us
  matrix products: 23.4 us -> 0 us
  starting transfers between devices: 17.1 us -> 0 us
  between operations: 16.6 us -> 4.35 us
    all_gather x1 -> x0, blocking collectives: 264 us -> none  [on_device(): past_rows = lax.all_gather(hyena_state, ('ctx', 'var'), axis=0, tiled=True)]
    another operation x4 -> x0, local copies, waits for them, and re-layouts: 79.1 us -> none  [on_device(): jnp.stack([lax.slice_in_dim(sequence, filter_len - offset, filter_len - o...]
    all_to_all x3 -> x0, waiting for transfers between devices: 76.7 us -> none  [the longest x1 66.8 us: on_device(): lax.all_to_all(numerators, 'ctx', split_axis=0, concat_axis=0, tiled=True)]
    pallas_call x0 -> x1, Pallas kernels: none -> 74.5 us  [on_device(): pl.pallas_call(functools.partial(spread_kernel, n, tp_count), out_shape=(...]
    psum x1 -> x0, waiting for transfers between devices: 50.9 us -> none  [on_device(): logits = lax.psum(logit_part, 'tp')]
    slice x7 -> x0, local copies, waits for them, and re-layouts: 39.5 us -> none  [the longest x6 32.7 us: on_device(): lax.slice_in_dim(sequence, filter_len - offset, filter_len - offset + pos...]
    reduce_sum x11 -> x0, other arithmetic: 26.1 us -> none  [the longest x3 10.3 us: summarize(): totals = weights.sum(-1)]
    dot_general x7 -> x0, matrix products: 23.4 us -> none  [the longest x3 11.8 us: summarize(): jnp.einsum('rhk,khd->rhd', weights.astype(jnp.bfloat16), values, preferre...]
  transfers between devices with their start and end apart: 6 -> 0, of which waited for: 4 -> 0; matrix products, arithmetic and copies ran while one was open for 29% -> 0% of each run, Pallas kernels for 0% -> 0%
where the time goes in v1:
time: 89.1 us; the launch traced here: 88.7 us
  Pallas kernels  74.5 us (84%)
  local copies, waits for them, and re-layouts  9.87 us (11%)
  between operations  4.35 us (5%)
    pallas_call x1, Pallas kernels, on_device(): pl.pallas_call(functools.partial(spread_kernel, n, tp_count), out_shape=(...  74.5 us
    unnamed x20, local copies, waits for them, and re-layouts  9.87 us

profile of v1, /device:TPU:1, one launch (start us, length us, event | category | flops | bytes accessed | tf_op | source)
XLA Modules:
  0.0 88.7 jit_solution(17212768219030768479)
XLA Ops:
  2.6 0.0 copy-start
  2.6 1.6 %copy-done = bf16[2048,512]{1,0:T(8,128)(2,1)S(1)} copy-done((bf16[2048,512]{1,0:T(8,128)(2,1)S(1)}, bf16[2048,512]{1,0:T(8,128)(2,1)}, u32[]{:S(2)}) %copy-start) | copy-done | bytes 2097176
  4.2 0.0 copy-start.1
  4.2 1.2 %copy-done.1 = f32[2048,128]{1,0:T(8,128)S(1)} copy-done((f32[2048,128]{1,0:T(8,128)S(1)}, f32[2048,128]{1,0:T(8,128)}, u32[]{:S(2)}) %copy-start.1) | copy-done | bytes 1048600
  5.4 0.0 copy-start.2
  5.4 1.0 %copy-done.2 = bf16[2,64,2048]{2,1,0:T(8,128)(2,1)S(1)} copy-done((bf16[2,64,2048]{2,1,0:T(8,128)(2,1)S(1)}, bf16[2,64,2048]{2,1,0:T(8,128)(2,1)}, u32[]{:S(2)}) %copy-start.2) | copy-done | bytes 524312
  6.4 0.0 copy-start.3
  6.4 1.0 %copy-done.3 = bf16[3,1,32,2048]{3,2,1,0:T(8,128)(2,1)S(1)} copy-done((bf16[3,1,32,2048]{3,2,1,0:T(8,128)(2,1)S(1)}, bf16[3,1,32,2048]{3,2,1,0:T(8,128)(2,1)}, u32[]{:S(2)}) %copy-start.3) | copy-done | bytes 393240
  7.4 0.0 copy-start.4
  7.4 0.9 %copy-done.4 = bf16[1,32,2048]{2,1,0:T(8,128)(2,1)S(1)} copy-done((bf16[1,32,2048]{2,1,0:T(8,128)(2,1)S(1)}, bf16[1,32,2048]{2,1,0:T(8,128)(2,1)}, u32[]{:S(2)}) %copy-start.4) | copy-done | bytes 131096
  8.3 0.0 copy-start.5
  8.3 0.9 %copy-done.5 = bf16[1,32,2048]{2,1,0:T(8,128)(2,1)S(1)} copy-done((bf16[1,32,2048]{2,1,0:T(8,128)(2,1)S(1)}, bf16[1,32,2048]{2,1,0:T(8,128)(2,1)}, u32[]{:S(2)}) %copy-start.5) | copy-done | bytes 131096
  9.2 0.0 copy-start.6
  9.2 0.7 copy-done.6
  9.9 0.0 copy-start.7
  9.9 0.7 copy-done.7
  10.6 0.0 copy-start.8
  10.6 0.7 copy-done.8
  11.3 74.5 %shard_map.139 = (bf16[1,32,2048]{2,1,0:T(8,128)(2,1)S(1)}, f32[1,32]{1,0:T(1,128)S(1)}, f32[1,1]{1,0:T(1,128)}) custom-call(bf16[2,64,2048]{2,1,0:T(8,128)(2,1)S(1)} %copy-done.2, bf16[1,32,2048]{2,1,0:T(8,128)(2,1)S(1)} %copy-done.4, bf16[1,32,2048]{2,1,0:T(8,128)(2,1)S(1)} %copy-done.5, bf16[3,1,32,2048]{3,2,1,0:T(8,128)(2,1)S(1)} %copy-done.3, ...), custom_call_target="tpu_custom_call" | custom-call | tf_op jit(solution)/shard_map/pallas_call | solution.py:754
  85.8 0.7 copy.21
  86.4 0.5 copy.22
Async XLA Ops:
  2.6 1.6 %copy-start = (bf16[2048,512]{1,0:T(8,128)(2,1)S(1)}, bf16[2048,512]{1,0:T(8,128)(2,1)}, u32[]{:S(2)}) copy-start(bf16[2048,512]{1,0:T(8,128)(2,1)} %unembed_ref.1) | copy-start | bytes 6291460
  4.2 1.2 %copy-start.1 = (f32[2048,128]{1,0:T(8,128)S(1)}, f32[2048,128]{1,0:T(8,128)}, u32[]{:S(2)}) copy-start(f32[2048,128]{1,0:T(8,128)} %filt_ref.1) | copy-start | bytes 3145732
  5.4 1.0 %copy-start.2 = (bf16[2,64,2048]{2,1,0:T(8,128)(2,1)S(1)}, bf16[2,64,2048]{2,1,0:T(8,128)(2,1)}, u32[]{:S(2)}) copy-start(bf16[2,64,2048]{2,1,0:T(8,128)(2,1)} %kv_ref.1) | copy-start | bytes 1572868
  6.4 1.0 %copy-start.3 = (bf16[3,1,32,2048]{3,2,1,0:T(8,128)(2,1)S(1)}, bf16[3,1,32,2048]{3,2,1,0:T(8,128)(2,1)}, u32[]{:S(2)}) copy-start(bf16[3,1,32,2048]{3,2,1,0:T(8,128)(2,1)} %hy_ref.1) | copy-start | bytes 1179652
  7.4 0.9 %copy-start.4 = (bf16[1,32,2048]{2,1,0:T(8,128)(2,1)S(1)}, bf16[1,32,2048]{2,1,0:T(8,128)(2,1)}, u32[]{:S(2)}) copy-start(bf16[1,32,2048]{2,1,0:T(8,128)(2,1)} %q_ref.1) | copy-start | bytes 393220
  8.3 0.9 %copy-start.5 = (bf16[1,32,2048]{2,1,0:T(8,128)(2,1)S(1)}, bf16[1,32,2048]{2,1,0:T(8,128)(2,1)}, u32[]{:S(2)}) copy-start(bf16[1,32,2048]{2,1,0:T(8,128)(2,1)} %ck_ref.1) | copy-start | bytes 393220
  9.2 0.7 copy-start.6
  9.9 0.7 copy-start.7
  10.6 0.7 copy-start.8

commit v2 on v1

v2 whole, which is shorter than its diff:
```python
import functools
import math

import jax
import jax.numpy as jnp
from jax import lax
from jax.experimental import pallas as pl
from jax.experimental.pallas import tpu as pltpu
from jax.sharding import PartitionSpec as P

HEAD_DIM = 128
BASE_TOKENS = (65, 67, 71, 84)
EXP_SCALE = HEAD_DIM ** (-0.5) * math.log2(math.e)
LOWEST = -3.0e38
BF16 = jnp.bfloat16
F32 = jnp.float32


def spread_kernel(
    n,
    tp_count,
    kv_ref,
    q_ref,
    ck_ref,
    hy_ref,
    state_ref,
    filt_ref,
    skip_ref,
    unembed_ref,
    bases_ref,
    pos_ref,
    allele_ref,
    length_ref,
    hyena_ref,
    log_probs_ref,
    score_ref,
    q_own,
    keys,
    values_own,
    values_t,
    state_src,
    state_all,
    state_rows,
    gathered,
    part_out,
    stat_out,
    part_in,
    stat_in,
    sum_numer,
    sum_stat,
    merged,
    merged_stat,
    back,
    back_stat,
    state_part,
    state_parts,
    stat_square,
    logit_parts,
    targets,
    padded,
    mixed,
    taps_own,
    q_v,
    kv_v,
    ck_v,
    hy_v,
    filt_v,
    unembed_v,
    state_v,
    skip_v,
    bases_s,
    pos_s,
    allele_s,
    length_s,
    local_sem,
    spread_send,
    spread_recv,
    gather_send,
    gather_recv,
    part_send,
    part_recv,
    stat_send,
    stat_recv,
    keys_send,
    keys_recv,
    values_send,
    values_recv,
    back_send,
    back_recv,
    tp_send,
    tp_recv,
):
    heads = 2 * n
    positions = q_v.shape[0]
    rows = heads * positions
    taps = filt_v.shape[1]
    channels = heads * HEAD_DIM
    vocab = unembed_v.shape[1]

    ctx = lax.axis_index("ctx")
    var = lax.axis_index("var")
    tp = lax.axis_index("tp")
    z = lax.div(ctx, 4)
    core = lax.rem(ctx, 2)
    y = var * 2 + lax.div(lax.rem(ctx, 4), 2)
    ring = (1 - core) * z + core * y
    other = (1 - core) * y + core * z
    head = (1 - core) * y + core * (n + z)

    def device(z_to, y_to, core_to):
        return {"ctx": z_to * 4 + lax.rem(y_to, 2) * 2 + core_to, "var": lax.div(y_to, 2)}

    def ring_device(offset):
        return device(
            lax.rem(z + offset * (1 - core), n), lax.rem(y + offset * core, n), core
        )

    sibling = device(z, y, 1 - core)

    def remote(src, dst, send_sem, recv_sem, device_id):
        return pltpu.make_async_remote_copy(
            src_ref=src,
            dst_ref=dst,
            send_sem=send_sem,
            recv_sem=recv_sem,
            device_id=device_id,
            device_id_type=pl.DeviceIdType.MESH,
        )

    def wait_for(ref, sem):
        pltpu.make_async_copy(ref, ref, sem).wait()

    def lanes_of(h):
        return pl.ds(pl.multiple_of(h * HEAD_DIM, HEAD_DIM), HEAD_DIM)

    barrier = pltpu.get_barrier_semaphore()

    def greet(device_id):
        pl.semaphore_signal(
            barrier, inc=1, device_id=device_id, device_id_type=pl.DeviceIdType.MESH
        )

    def greet_offset(k, carry):
        for core_to in range(2):
            greet(device(z, lax.rem(y + k, n), core_to))
            greet(device(lax.rem(z + k, n), y, core_to))
        return carry

    lax.fori_loop(1, n, greet_offset, 0)
    greet(sibling)
    for k in range(1, tp_count):
        greet({"tp": lax.rem(tp + k, tp_count)})

    small = [
        pltpu.make_async_copy(src, dst, local_sem.at[8 + i])
        for i, (src, dst) in enumerate(
            (
                (state_ref, state_v),
                (skip_ref, skip_v),
                (bases_ref, bases_s),
                (pos_ref, pos_s),
                (allele_ref, allele_s),
                (length_ref, length_s),
            )
        )
    ]
    for load in small:
        load.start()
    load_q = pltpu.make_async_copy(q_ref.at[0], q_v, local_sem.at[2])
    load_kv = pltpu.make_async_copy(kv_ref, kv_v, local_sem.at[14])
    load_hyena = pltpu.make_async_copy(hy_ref.at[:, 0], hy_v, local_sem.at[0])
    load_filter = pltpu.make_async_copy(filt_ref, filt_v, local_sem.at[1])
    load_keys = pltpu.make_async_copy(ck_ref.at[0], ck_v, local_sem.at[3])
    load_unembed = pltpu.make_async_copy(unembed_ref, unembed_v, local_sem.at[4])
    for load in (load_q, load_kv, load_hyena, load_filter, load_keys, load_unembed):
        load.start()

    small[0].wait()
    for h in range(heads):
        state_src[h] = state_v[:, h * HEAD_DIM : (h + 1) * HEAD_DIM].astype(F32)
    load_q.wait()
    load_kv.wait()
    pl.semaphore_wait(barrier, 4 * (n - 1) + 1 + tp_count - 1)

    slot_y = 2 * y + core
    slot_z = 2 * z + core
    slot_self = 2 * other + core
    slot_sibling = 2 * ring + core
    head_sibling = (1 - core) * (n + z) + core * y

    def q_copy(h, slot, device_id):
        return remote(
            q_v.at[:, lanes_of(h)],
            q_own.at[slot],
            spread_send.at[0],
            spread_recv.at[0],
            device_id,
        )

    def state_copy(h, ring_to, slot, device_id):
        return remote(
            state_src.at[h],
            state_all.at[ring_to, slot],
            spread_send.at[1],
            spread_recv.at[1],
            device_id,
        )

    def keys_copy(h, slot, device_id):
        return remote(
            kv_v.at[0, :, lanes_of(h)],
            keys.at[1, slot],
            spread_send.at[2],
            spread_recv.at[2],
            device_id,
        )

    def values_copy(h, slot, device_id):
        return remote(
            kv_v.at[1, :, lanes_of(h)],
            values_own.at[slot],
            spread_send.at[4],
            spread_recv.at[4],
            device_id,
        )

    def send_all(copy):
        def send(k, carry):
            y_to = lax.rem(y + k, n)
            z_to = lax.rem(z + k, n)
            copy(y_to, slot_y, device(z, y_to, 0)).start()
            copy(n + z_to, slot_z, device(z_to, y, 1)).start()
            return carry

        lax.fori_loop(1, n, send, 0)
        copy(head_sibling, slot_sibling, sibling).start()

    def send_state(k, carry):
        y_to = lax.rem(y + k, n)
        z_to = lax.rem(z + k, n)
        state_copy(y_to, z, slot_y, device(z, y_to, 0)).start()
        state_copy(n + z_to, y, slot_z, device(z_to, y, 1)).start()
        return carry

    self_q = pltpu.make_async_copy(
        q_v.at[:, lanes_of(head)], q_own.at[slot_self], local_sem.at[5]
    )
    self_keys = pltpu.make_async_copy(
        kv_v.at[0, :, lanes_of(head)], keys.at[1, slot_self], local_sem.at[6]
    )
    self_values = pltpu.make_async_copy(
        kv_v.at[1, :, lanes_of(head)], values_own.at[slot_self], local_sem.at[15]
    )
    self_state = pltpu.make_async_copy(
        state_src.at[head], state_all.at[ring, slot_self], local_sem.at[7]
    )
    send_all(q_copy)
    self_q.start()
    lax.fori_loop(1, n, send_state, 0)
    state_copy(head_sibling, other, slot_sibling, sibling).start()
    self_state.start()
    send_all(keys_copy)
    self_keys.start()
    send_all(values_copy)
    self_values.start()

    load_hyena.wait()
    product = (hy_v[1].astype(F32) * hy_v[2].astype(F32)).astype(BF16).astype(F32)
    padded[0:positions, :] = jnp.zeros((positions, channels), F32)
    padded[positions:, :] = product
    for load in small[1:]:
        load.wait()
    mixed[...] = skip_v[...] * product
    row_index = lax.broadcasted_iota(jnp.int32, (positions, vocab), 0)
    codes = jnp.zeros((positions, vocab), jnp.int32)
    for t in range(positions):
        codes = jnp.where(row_index == t, bases_s[t], codes)
    codes = jnp.where(row_index == pos_s[0], allele_s[0], codes)
    wanted = jnp.zeros((positions, vocab), jnp.int32)
    for code, token in enumerate(BASE_TOKENS):
        wanted = jnp.where(codes == code, token, wanted)
    targets[...] = wanted

    away = (3, n - 3)

    def gather_copy(side):
        return remote(
            q_own,
            gathered.at[side],
            gather_send.at[side],
            gather_recv.at[side],
            ring_device(away[side]),
        )

    wait_for(q_own.at[0 : heads - 1], spread_recv.at[0])
    self_q.wait()
    for side in range(2):
        gather_copy(side).start()

    wait_for(state_all.at[0, 0 : heads - 1], spread_recv.at[1])
    self_state.wait()
    state_mine = state_all.at[ring]

    def send_state_on(k, carry):
        remote(
            state_mine, state_mine, spread_send.at[3], spread_recv.at[3], ring_device(k)
        ).start()
        return carry

    lax.fori_loop(1, n, send_state_on, 0)

    load_filter.wait()

    def own_taps(h, carry):
        lanes = lanes_of(h)
        coeffs = jnp.transpose(filt_v[lanes, :])
        total = mixed[:, lanes]
        for j in range(1, positions):
            total = total + padded[positions - j : 2 * positions - j, lanes] * coeffs[j - 1 : j, :]
        mixed[:, lanes] = total
        return carry

    lax.fori_loop(0, heads, own_taps, 0)

    right = ring_device(1)
    left = ring_device(n - 1)

    def exchange(ref, send_sem, recv_sem):
        return (
            remote(ref.at[1], ref.at[0], send_sem.at[0], recv_sem.at[0], right),
            remote(ref.at[1], ref.at[2], send_sem.at[1], recv_sem.at[1], left),
        )

    wait_for(keys.at[1, 0 : heads - 1], spread_recv.at[2])
    self_keys.wait()
    keys_on = exchange(keys, keys_send, keys_recv)
    for copy in keys_on:
        copy.start()

    wait_for(values_own.at[0 : heads - 1], spread_recv.at[4])
    self_values.wait()
    block = values_own.shape[1]
    context = heads * block
    values_t[1] = jnp.transpose(values_own[...].reshape(context, HEAD_DIM))
    values_on = exchange(values_t, values_send, values_recv)
    for copy in values_on:
        copy.start()

    taps_own[...] = jnp.transpose(filt_v[lanes_of(head), :])
    state_rows[taps:, :] = jnp.zeros((positions, HEAD_DIM), F32)
    wait_for(state_all.at[0 : n - 1], spread_recv.at[3])

    for at in range(n):
        for slot in range(heads):
            spot, bit = divmod(slot, 2)
            row_z = (4 * at + 2 * (spot % 2) + bit) * (n // 2) + spot // 2
            row_y = (4 * spot + 2 * (at % 2) + bit) * (n // 2) + at // 2
            row = row_z + core * (row_y - row_z)
            state_rows[pl.ds(row, 1), :] = state_all[at, slot]

    def state_taps(step, total):
        base = pl.multiple_of(step * 8, 8)
        for b in range(8):
            total = total + (
                state_rows[pl.ds(base + b, positions), :]
                * taps_own[pl.ds(taps - 1 - b - base, 1), :]
            )
        return total

    state_part[...] = lax.fori_loop(
        0, taps // 8, state_taps, jnp.zeros((positions, HEAD_DIM), F32)
    ).astype(BF16)

    def back_device(k, core_to):
        spot = lax.rem(other + k, n)
        return (
            2 * spot + core_to,
            device((1 - core) * z + core * spot, (1 - core) * spot + core * y, core_to),
        )

    slot_beside = 2 * other + 1 - core

    def state_back(device_id):
        return remote(
            state_part, state_parts.at[head], back_send.at[0], back_recv.at[0], device_id
        )

    def send_state_back(k, carry):
        for core_to in range(2):
            state_back(back_device(k, core_to)[1]).start()
        return carry

    lax.fori_loop(1, n, send_state_back, 0)
    state_back(sibling).start()
    state_parts[head] = state_part[...]

    def merge(a, b):
        peak = jnp.maximum(a[1], b[1])
        scale_a = jnp.exp2((a[1] - peak) * EXP_SCALE)
        scale_b = jnp.exp2((b[1] - peak) * EXP_SCALE)
        return (a[0] * scale_a + b[0] * scale_b, peak, a[2] * scale_a + b[2] * scale_b)

    def attend(chunk, place, first=0, last=heads):
        from_keys = keys[place, first:last].reshape((last - first) * block, HEAD_DIM)
        from_values = values_t[place, :, first * block : last * block]
        numer, peak, total = [], [], []
        width = min(256, rows)
        for start in range(0, rows, width):
            part = chunk[start : start + width]
            scores = lax.dot_general(
                from_keys, part, (((1,), (1,)), ((), ())), preferred_element_type=F32
            )
            top = jnp.max(scores, 0, keepdims=True)
            weights = jnp.exp2((scores - top) * EXP_SCALE)
            peak.append(top)
            total.append(jnp.sum(weights, 0, keepdims=True))
            numer.append(jnp.dot(from_values, weights.astype(BF16), preferred_element_type=F32))
        return (
            jnp.concatenate(numer, 1),
            jnp.concatenate(peak, 1),
            jnp.concatenate(total, 1),
        )

    def chunk_of(index):
        ref = q_own if index == 2 else gathered.at[index]
        return ref[...].reshape(rows, HEAD_DIM)

    def store_sums(index, sums):
        sum_numer[index] = sums[0]
        sum_stat[index, 0:1, :] = sums[1]
        sum_stat[index, 1:2, :] = sums[2]

    def load_sums(index):
        return (sum_numer[index], sum_stat[index, 0:1, :], sum_stat[index, 1:2, :])

    store_sums(2, attend(chunk_of(2), 1))
    for side in range(2):
        gather_copy(side).wait_recv()
        store_sums(side, attend(chunk_of(side), 1))

    def part_copy(side):
        return remote(
            part_out.at[side],
            part_in.at[side],
            part_send.at[side],
            part_recv.at[side],
            ring_device(away[1 - side]),
        )

    def stat_copy(side):
        return remote(
            stat_out.at[side],
            stat_in.at[side],
            stat_send.at[side],
            stat_recv.at[side],
            ring_device(away[1 - side]),
        )

    for copy in keys_on + values_on:
        copy.wait_recv()
    middle = heads // 2
    for side in range(2):
        near_place, far_place = (0, 2) if side == 0 else (2, 0)
        far_first, far_last = (0, middle) if side == 0 else (middle, heads)
        sums = merge(load_sums(side), attend(chunk_of(side), near_place))
        sums = merge(sums, attend(chunk_of(side), far_place, far_first, far_last))
        part_out[side] = sums[0].astype(BF16)
        stat_out[side, 0:1, :] = sums[1]
        stat_out[side, 1:2, :] = sums[2]
        part_copy(side).start()
        stat_copy(side).start()
    sums = merge(load_sums(2), attend(chunk_of(2), 0))
    store_sums(2, merge(sums, attend(chunk_of(2), 2)))

    wait_for(state_parts.at[0 : heads - 1], back_recv.at[0])
    for h in range(heads):
        lanes = slice(h * HEAD_DIM, (h + 1) * HEAD_DIM)
        hyena_ref[0, :, lanes] = (
            hy_v[0, :, lanes].astype(F32) * (mixed[:, lanes] + state_parts[h].astype(F32))
        ).astype(BF16)
    load_keys.wait()
    group = HEAD_DIM // positions
    own = []
    row_at = lax.broadcasted_iota(jnp.int32, (HEAD_DIM, HEAD_DIM), 0)
    col_at = lax.broadcasted_iota(jnp.int32, (HEAD_DIM, HEAD_DIM), 1)
    seen = (lax.div(row_at, positions) == lax.div(col_at, positions)) & (col_at <= row_at)

    def stacked(ref, g):
        return jnp.concatenate(
            [ref[:, h * HEAD_DIM : (h + 1) * HEAD_DIM] for h in range(g * group, (g + 1) * group)],
            0,
        )

    for g in range(heads // group):
        scores = lax.dot_general(
            stacked(q_v, g), stacked(ck_v, g), (((1,), (1,)), ((), ())), preferred_element_type=F32
        )
        scores = jnp.where(seen, scores, LOWEST)
        top = jnp.max(scores, 1, keepdims=True)
        weights = jnp.where(seen, jnp.exp2((scores - top) * EXP_SCALE), 0.0)
        total = jnp.sum(weights, 1, keepdims=True)
        numer = jnp.dot(
            weights.astype(BF16), stacked(hyena_ref.at[0], g), preferred_element_type=F32
        )
        own.append((numer, top, total))

    mine = load_sums(2)
    for side in range(2):
        part_copy(side).wait_recv()
        stat_copy(side).wait_recv()
        mine = merge(
            mine,
            (part_in[side].astype(F32), stat_in[side, 0:1, :], stat_in[side, 1:2, :]),
        )
    numer, peak, total = mine
    merged[...] = jnp.transpose(numer).astype(BF16).reshape(merged.shape)
    for b in range(rows // HEAD_DIM):
        merged_stat[b, 0:1, :] = peak[:, b * HEAD_DIM : (b + 1) * HEAD_DIM]
        merged_stat[b, 1:2, :] = total[:, b * HEAD_DIM : (b + 1) * HEAD_DIM]

    def back_copy(slot, device_id):
        return remote(
            merged.at[slot], back.at[head], back_send.at[1], back_recv.at[1], device_id
        )

    def back_stat_copy(slot, device_id):
        return remote(
            merged_stat.at[lax.div(slot, group)],
            back_stat.at[head],
            back_send.at[2],
            back_recv.at[2],
            device_id,
        )

    def send_back(k, carry):
        for core_to in range(2):
            slot, device_id = back_device(k, core_to)
            back_copy(slot, device_id).start()
            back_stat_copy(slot, device_id).start()
        return carry

    lax.fori_loop(1, n, send_back, 0)
    back_copy(slot_beside, sibling).start()
    back_stat_copy(slot_beside, sibling).start()
    back[head] = merged[slot_self]
    back_stat[head] = merged_stat[lax.div(slot_self, group)]

    load_unembed.wait()
    stat_square[...] = jnp.zeros_like(stat_square)
    wait_for(back_stat.at[0 : heads - 1], back_recv.at[2])
    for first, slot in ((0, slot_y), (n, slot_z)):
        shift = lax.rem(HEAD_DIM - lax.rem(slot, group) * positions, HEAD_DIM)
        for kind in range(2):
            stat_square[kind * heads + first : kind * heads + first + n, :] = pltpu.roll(
                back_stat[first : first + n, kind, :], shift, 1
            )
    columns = jnp.transpose(stat_square[...])
    wait_for(back.at[0 : heads - 1], back_recv.at[1])
    pieces = []
    for g in range(heads // group):
        chosen = range(g * group, (g + 1) * group)
        peak = jnp.concatenate([columns[0:positions, h : h + 1] for h in chosen], 0)
        total = jnp.concatenate(
            [columns[0:positions, heads + h : heads + h + 1] for h in chosen], 0
        )
        numer = back[g * group : (g + 1) * group].reshape(HEAD_DIM, HEAD_DIM).astype(F32)
        numer, _, total = merge((numer, peak, total), own[g])
        attended = numer / total
        pieces += [attended[i * positions : (i + 1) * positions] for i in range(group)]
    attended = jnp.concatenate(pieces, 1)
    high = attended.astype(BF16)
    low = (attended - high.astype(F32)).astype(BF16)
    both = jnp.dot(
        jnp.concatenate([high, low], 0), unembed_v[...], preferred_element_type=F32
    )
    logit_parts[tp] = (both[0:positions] + both[positions:]).astype(BF16)

    tp_copies = [
        remote(
            logit_parts.at[tp],
            logit_parts.at[tp],
            tp_send,
            tp_recv,
            {"tp": lax.rem(tp + k, tp_count)},
        )
        for k in range(1, tp_count)
    ]
    for copy in tp_copies:
        copy.start()
    if tp_count > 1:
        wait_for(logit_parts.at[0 : tp_count - 1], tp_recv)
    logits = logit_parts[0].astype(F32)
    for k in range(1, tp_count):
        logits = logits + logit_parts[k].astype(F32)
    top = jnp.max(logits, 1, keepdims=True)
    log_total = top + jnp.log(jnp.sum(jnp.exp(logits - top), 1, keepdims=True))
    vocab_at = lax.broadcasted_iota(jnp.int32, (positions, vocab), 1)
    picked = jnp.sum(jnp.where(vocab_at == targets[...], logits, 0.0), 1, keepdims=True)
    log_probs = picked - log_total
    place = lax.broadcasted_iota(jnp.int32, (positions, positions), 0)
    lane = lax.broadcasted_iota(jnp.int32, (positions, positions), 1)
    log_row = jnp.sum(jnp.where(place == lane, log_probs, 0.0), 0, keepdims=True)
    log_probs_ref[...] = log_row
    lane_row = lax.broadcasted_iota(jnp.int32, (1, positions), 1)
    score_ref[...] = jnp.sum(
        jnp.where(lane_row < length_s[0], log_row, 0.0), 1, keepdims=True
    )

    wait_for(q_own.at[0 : heads - 1], spread_send.at[0])
    wait_for(state_all.at[0, 0 : heads - 1], spread_send.at[1])
    wait_for(keys.at[1, 0 : heads - 1], spread_send.at[2])
    wait_for(values_own.at[0 : heads - 1], spread_send.at[4])
    wait_for(state_all.at[0 : n - 1], spread_send.at[3])
    for copy in keys_on + values_on:
        copy.wait_send()
    for side in range(2):
        gather_copy(side).wait_send()
        part_copy(side).wait_send()
        stat_copy(side).wait_send()
    wait_for(state_parts.at[0 : heads - 1], back_send.at[0])
    wait_for(back.at[0 : heads - 1], back_send.at[1])
    wait_for(back_stat.at[0 : heads - 1], back_send.at[2])
    if tp_count > 1:
        wait_for(logit_parts.at[0 : tp_count - 1], tp_send)


def on_device(
    n,
    tp_count,
    context_kv,
    queries,
    cont_keys,
    hyena_inputs,
    hyena_state,
    hyena_filter,
    filter_skip,
    unembed,
    ref_bases,
    variant_pos,
    allele_ids,
    cont_lengths,
):
    positions, channels = queries.shape[1:]
    block = context_kv.shape[1]
    taps = hyena_filter.shape[1]
    vocab = unembed.shape[1]
    heads = channels // HEAD_DIM
    rows = heads * positions
    vmem = pltpu.VMEM
    dma = pltpu.SemaphoreType.DMA
    scratch = [
        vmem((heads, positions, HEAD_DIM), BF16),
        vmem((3, heads, block, HEAD_DIM), BF16),
        vmem((heads, block, HEAD_DIM), BF16),
        vmem((3, HEAD_DIM, heads * block), BF16),
        vmem((heads, 1, HEAD_DIM), F32),
        vmem((n, heads, 1, HEAD_DIM), F32),
        vmem((taps + positions, HEAD_DIM), F32),
        vmem((2, heads, positions, HEAD_DIM), BF16),
        vmem((2, HEAD_DIM, rows), BF16),
        vmem((2, 2, rows), F32),
        vmem((2, HEAD_DIM, rows), BF16),
        vmem((2, 2, rows), F32),
        vmem((3, HEAD_DIM, rows), F32),
        vmem((3, 2, rows), F32),
        vmem((heads, positions, HEAD_DIM), BF16),
        vmem((rows // HEAD_DIM, 2, HEAD_DIM), F32),
        vmem((heads, positions, HEAD_DIM), BF16),
        vmem((heads, 2, HEAD_DIM), F32),
        vmem((positions, HEAD_DIM), BF16),
        vmem((heads, positions, HEAD_DIM), BF16),
        vmem((HEAD_DIM, HEAD_DIM), F32),
        vmem((tp_count, positions, vocab), BF16),
        vmem((positions, vocab), jnp.int32),
        vmem((2 * positions, channels), F32),
        vmem((positions, channels), F32),
        vmem((taps, HEAD_DIM), F32),
        vmem((positions, channels), BF16),
        vmem((2, block, channels), BF16),
        vmem((positions, channels), BF16),
        vmem((3, positions, channels), BF16),
        vmem((channels, taps), F32),
        vmem((channels, vocab), BF16),
        vmem((1, channels), BF16),
        vmem((1, channels), F32),
        pltpu.SMEM((positions,), jnp.int32),
        pltpu.SMEM((1,), jnp.int32),
        pltpu.SMEM((1,), jnp.int32),
        pltpu.SMEM((1,), jnp.int32),
        dma((16,)),
        dma((5,)),
        dma((5,)),
        dma((2,)),
        dma((2,)),
        dma((2,)),
        dma((2,)),
        dma((2,)),
        dma((2,)),
        dma((2,)),
        dma((2,)),
        dma((2,)),
        dma((2,)),
        dma((3,)),
        dma((3,)),
        dma,
        dma,
    ]
    hbm = pl.BlockSpec(memory_space=pltpu.HBM)
    in_vmem = pl.BlockSpec(memory_space=pltpu.VMEM)
    hyena_out, log_probs, score = pl.pallas_call(
        functools.partial(spread_kernel, n, tp_count),
        out_shape=(
            jax.ShapeDtypeStruct((1, positions, channels), BF16),
            jax.ShapeDtypeStruct((1, positions), F32),
            jax.ShapeDtypeStruct((1, 1), F32),
        ),
        in_specs=[hbm] * 12,
        out_specs=(in_vmem, in_vmem, in_vmem),
        scratch_shapes=scratch,
        compiler_params=pltpu.CompilerParams(
            collective_id=0, has_side_effects=True, vmem_limit_bytes=60 * 1024 * 1024
        ),
    )(
        context_kv,
        queries,
        cont_keys,
        hyena_inputs,
        hyena_state,
        hyena_filter,
        filter_skip.reshape(1, channels),
        unembed,
        ref_bases,
        variant_pos,
        allele_ids,
        cont_lengths,
    )
    return hyena_out, log_probs, score.reshape(1)


def solution(mesh):
    n = mesh.shape["ctx"] // 4
    placed = (
        P(None, ("ctx", "var"), "tp"),
        P(("ctx", "var"), None, "tp"),
        P(("ctx", "var"), None, "tp"),
        P(None, ("ctx", "var"), None, "tp"),
        P(("ctx", "var"), "tp"),
        P("tp", None),
        P("tp"),
        P("tp", None),
        P(),
        P(("ctx", "var")),
        P(("ctx", "var")),
        P(("ctx", "var")),
    )
    return jax.shard_map(
        functools.partial(on_device, n, mesh.shape["tp"]),
        mesh=mesh,
        in_specs=placed,
        out_specs=(P(("ctx", "var"), None, "tp"), P(("ctx", "var"), None), P(("ctx", "var"))),
        check_vma=False,
    )
```

time: 89.1 us -> 67.3 us (0.76)
  Pallas kernels: 74.5 us -> 60 us
  local copies, waits for them, and re-layouts: 9.87 us -> 2.74 us
    pallas_call x1, Pallas kernels: 74.5 us -> 60 us  [on_device(): pl.pallas_call(functools.partial(spread_kernel, n, tp_count), out_shape=(...]
    unnamed x20 -> x2, local copies, waits for them, and re-layouts: 9.87 us -> 2.74 us
where the time goes in v2:
time: 67.3 us; the launch traced here: 67.1 us
  Pallas kernels  60 us (89%)
  between operations  4.33 us (6%)
  local copies, waits for them, and re-layouts  2.74 us (4%)
    pallas_call x1, Pallas kernels, on_device(): pl.pallas_call(functools.partial(spread_kernel, n, tp_count), out_shape=(...  60 us
    unnamed x2, local copies, waits for them, and re-layouts  2.74 us

profile of v2, /device:TPU:1, one launch (start us, length us, event | category | flops | bytes accessed | tf_op | source)
XLA Modules:
  0.0 67.1 jit_solution(18348989757857879331)
XLA Ops:
  2.6 60.0 %shard_map.139 = (bf16[1,32,2048]{2,1,0:T(8,128)(2,1)}, f32[1,32]{1,0:T(1,128)}, f32[1,1]{1,0:T(1,128)}) custom-call(bf16[2,64,2048]{2,1,0:T(8,128)(2,1)} %kv_ref.1, bf16[1,32,2048]{2,1,0:T(8,128)(2,1)} %q_ref.1, bf16[1,32,2048]{2,1,0:T(8,128)(2,1)} %ck_ref.1, bf16[3,1,32,2048]{3,2,1,0:T(8,128)(2,1)} %hy_ref.1, bf16[1,2048]{1,0:T(2,128)(2,1)} %state_ref.1, ...), custom_call_target="tpu_custom_call" | custom-call | tf_op jit(solution)/shard_map/pallas_call | solution.py:710
  62.6 1.6 %copy.21 = bf16[1,32,2048]{2,1,0:T(8,128)(2,1)} copy(bf16[1,32,2048]{2,1,0:T(8,128)(2,1)} %get-tuple-element.12) | data formatting | bytes 262144
  64.1 1.2 %copy.22 = f32[1,32]{1,0:T(1,128)} copy(f32[1,32]{1,0:T(1,128)} %get-tuple-element.13) | data formatting | bytes 256

commit v3 on v2

--- a/solution.py
+++ b/solution.py
@@ -48,6 +48,7 @@
     stat_in,
     sum_numer,
     sum_stat,
+    weights_kept,
     merged,
     merged_stat,
     back,
@@ -400,10 +401,9 @@
         scale_b = jnp.exp2((b[1] - peak) * EXP_SCALE)
         return (a[0] * scale_a + b[0] * scale_b, peak, a[2] * scale_a + b[2] * scale_b)
 
-    def attend(chunk, place, first=0, last=heads):
+    def weigh(chunk, place, first=0, last=heads):
         from_keys = keys[place, first:last].reshape((last - first) * block, HEAD_DIM)
-        from_values = values_t[place, :, first * block : last * block]
-        numer, peak, total = [], [], []
+        weights, peak, total = [], [], []
         width = min(256, rows)
         for start in range(0, rows, width):
             part = chunk[start : start + width]
@@ -411,15 +411,19 @@
                 from_keys, part, (((1,), (1,)), ((), ())), preferred_element_type=F32
             )
             top = jnp.max(scores, 0, keepdims=True)
-            weights = jnp.exp2((scores - top) * EXP_SCALE)
+            weight = jnp.exp2((scores - top) * EXP_SCALE)
+            weights.append(weight.astype(BF16))
             peak.append(top)
-            total.append(jnp.sum(weights, 0, keepdims=True))
-            numer.append(jnp.dot(from_values, weights.astype(BF16), preferred_element_type=F32))
-        return (
-            jnp.concatenate(numer, 1),
-            jnp.concatenate(peak, 1),
-            jnp.concatenate(total, 1),
-        )
+            total.append(jnp.sum(weight, 0, keepdims=True))
+        return [jnp.concatenate(pieces, 1) for pieces in (weights, peak, total)]
+
+    def apply(weights, place, first=0, last=heads):
+        from_values = values_t[place, :, first * block : last * block]
+        return jnp.dot(from_values, weights, preferred_element_type=F32)
+
+    def attend(chunk, place):
+        weights, peak, total = weigh(chunk, place)
+        return apply(weights, place), peak, total
 
     def chunk_of(index):
         ref = q_own if index == 2 else gathered.at[index]
@@ -433,7 +437,6 @@
     def load_sums(index):
         return (sum_numer[index], sum_stat[index, 0:1, :], sum_stat[index, 1:2, :])
 
-    store_sums(2, attend(chunk_of(2), 1))
     for side in range(2):
         gather_copy(side).wait_recv()
         store_sums(side, attend(chunk_of(side), 1))
@@ -456,21 +459,42 @@
             ring_device(away[1 - side]),
         )
 
-    for copy in keys_on + values_on:
+    middle = heads // 2
+    spans = (
+        ((0, 0, heads), (2, 0, middle)),
+        ((2, 0, heads), (0, middle, heads)),
+        ((0, 0, heads), (2, 0, heads)),
+    )
+    for copy in keys_on:
         copy.wait_recv()
-    middle = heads // 2
+    stats = []
+    for index in range(2):
+        for which, (place, first, last) in enumerate(spans[index]):
+            weights, peak, total = weigh(chunk_of(index), place, first, last)
+            weights_kept[index, which, 0 : (last - first) * block, :] = weights
+            stats.append((peak, total))
+
+    def finish(index):
+        sums = load_sums(index)
+        for which, (place, first, last) in enumerate(spans[index]):
+            numer = apply(
+                weights_kept[index, which, 0 : (last - first) * block, :], place, first, last
+            )
+            sums = merge(sums, (numer, *stats[2 * index + which]))
+        return sums
+
+    for copy in values_on:
+        copy.wait_recv()
     for side in range(2):
-        near_place, far_place = (0, 2) if side == 0 else (2, 0)
-        far_first, far_last = (0, middle) if side == 0 else (middle, heads)
-        sums = merge(load_sums(side), attend(chunk_of(side), near_place))
-        sums = merge(sums, attend(chunk_of(side), far_place, far_first, far_last))
+        sums = finish(side)
         part_out[side] = sums[0].astype(BF16)
         stat_out[side, 0:1, :] = sums[1]
         stat_out[side, 1:2, :] = sums[2]
         part_copy(side).start()
         stat_copy(side).start()
-    sums = merge(load_sums(2), attend(chunk_of(2), 0))
-    store_sums(2, merge(sums, attend(chunk_of(2), 2)))
+    store_sums(2, attend(chunk_of(2), 1))
+    for place, first, last in spans[2]:
+        store_sums(2, merge(load_sums(2), attend(chunk_of(2), place)))
 
     wait_for(state_parts.at[0 : heads - 1], back_recv.at[0])
     for h in range(heads):
@@ -663,6 +687,7 @@
         vmem((2, 2, rows), F32),
         vmem((3, HEAD_DIM, rows), F32),
         vmem((3, 2, rows), F32),
+        vmem((3, 2, heads * block, rows), BF16),
         vmem((heads, positions, HEAD_DIM), BF16),
         vmem((rows // HEAD_DIM, 2, HEAD_DIM), F32),
         vmem((heads, positions, HEAD_DIM), BF16),
@@ -707,6 +732,20 @@
     ]
     hbm = pl.BlockSpec(memory_space=pltpu.HBM)
     in_vmem = pl.BlockSpec(memory_space=pltpu.VMEM)
+    stay = [
+        pltpu.with_memory_space_constraint(array, pltpu.HBM)
+        for array in (
+            context_kv,
+            queries,
+            cont_keys,
+            hyena_inputs,
+            hyena_state,
+            hyena_filter,
+            filter_skip.reshape(1, channels),
+            unembed,
+            ref_bases,
+        )
+    ]
     hyena_out, log_probs, score = pl.pallas_call(
         functools.partial(spread_kernel, n, tp_count),
         out_shape=(
@@ -718,18 +757,10 @@
         out_specs=(in_vmem, in_vmem, in_vmem),
         scratch_shapes=scratch,
         compiler_params=pltpu.CompilerParams(
-            collective_id=0, has_side_effects=True, vmem_limit_bytes=60 * 1024 * 1024
+            collective_id=0, has_side_effects=True, vmem_limit_bytes=48 * 1024 * 1024
         ),
     )(
-        context_kv,
-        queries,
-        cont_keys,
-        hyena_inputs,
-        hyena_state,
-        hyena_filter,
-        filter_skip.reshape(1, channels),
-        unembed,
-        ref_bases,
+        *stay,
         variant_pos,
         allele_ids,
         cont_lengths,

time: 67.3 us -> 61.6 us (0.915); the launches traced: 67.1 us -> 60.6 us
  Pallas kernels: 60 us -> 55.2 us
  local copies, waits for them, and re-layouts: 2.74 us -> 1.17 us
    pallas_call x1, Pallas kernels: 60 us -> 55.2 us  [on_device(): pl.pallas_call(functools.partial(spread_kernel, n, tp_count), out_shape=(...]
    unnamed x2, local copies, waits for them, and re-layouts: 2.74 us -> 1.17 us
where the time goes in v3:
time: 61.6 us; the launch traced here: 60.6 us
  Pallas kernels  55.2 us (90%)
  between operations  4.27 us (7%)
  local copies, waits for them, and re-layouts  1.17 us (2%)
    pallas_call x1, Pallas kernels, on_device(): pl.pallas_call(functools.partial(spread_kernel, n, tp_count), out_shape=(...  55.2 us

profile of v3, /device:TPU:1, one launch (start us, length us, event | category | flops | bytes accessed | tf_op | source)
XLA Modules:
  0.0 60.6 jit_solution(6640088640268946749)
XLA Ops:
  2.6 55.2 %shard_map.139 = (bf16[1,32,2048]{2,1,0:T(8,128)(2,1)S(1)}, f32[1,32]{1,0:T(1,128)S(1)}, f32[1,1]{1,0:T(1,128)}) custom-call(bf16[2,64,2048]{2,1,0:T(8,128)(2,1)} %kv_ref.1, bf16[1,32,2048]{2,1,0:T(8,128)(2,1)} %q_ref.1, bf16[1,32,2048]{2,1,0:T(8,128)(2,1)} %ck_ref.1, bf16[3,1,32,2048]{3,2,1,0:T(8,128)(2,1)} %hy_ref.1, bf16[1,2048]{1,0:T(2,128)(2,1)} %state_ref.1, ...), custom_call_target="tpu_custom_call" | custom-call | tf_op jit(solution)/shard_map/pallas_call | solution.py:749
  57.8 0.7 %copy.21 = bf16[1,32,2048]{2,1,0:T(8,128)(2,1)} copy(bf16[1,32,2048]{2,1,0:T(8,128)(2,1)S(1)} %get-tuple-element.12) | data formatting | bytes 262144
  58.4 0.5 copy.22

commit v4 on v3

--- a/solution.py
+++ b/solution.py
@@ -95,6 +95,7 @@
     positions = q_v.shape[0]
     rows = heads * positions
     taps = filt_v.shape[1]
+    group = HEAD_DIM // positions
     channels = heads * HEAD_DIM
     vocab = unembed_v.shape[1]
 
@@ -131,6 +132,13 @@
     def wait_for(ref, sem):
         pltpu.make_async_copy(ref, ref, sem).wait()
 
+    def farthest_first(send):
+        def at(index, carry):
+            step = lax.div(index + 1, 2) * (2 * lax.rem(index, 2) - 1)
+            return send(n // 2 + step, carry)
+
+        lax.fori_loop(0, n - 1, at, 0)
+
     def lanes_of(h):
         return pl.ds(pl.multiple_of(h * HEAD_DIM, HEAD_DIM), HEAD_DIM)
 
@@ -147,7 +155,7 @@
             greet(device(lax.rem(z + k, n), y, core_to))
         return carry
 
-    lax.fori_loop(1, n, greet_offset, 0)
+    farthest_first(greet_offset)
     greet(sibling)
     for k in range(1, tp_count):
         greet({"tp": lax.rem(tp + k, tp_count)})
@@ -233,7 +241,7 @@
             copy(n + z_to, slot_z, device(z_to, y, 1)).start()
             return carry
 
-        lax.fori_loop(1, n, send, 0)
+        farthest_first(send)
         copy(head_sibling, slot_sibling, sibling).start()
 
     def send_state(k, carry):
@@ -257,7 +265,7 @@
     )
     send_all(q_copy)
     self_q.start()
-    lax.fori_loop(1, n, send_state, 0)
+    farthest_first(send_state)
     state_copy(head_sibling, other, slot_sibling, sibling).start()
     self_state.start()
     send_all(keys_copy)
@@ -282,34 +290,6 @@
         wanted = jnp.where(codes == code, token, wanted)
     targets[...] = wanted
 
-    away = (3, n - 3)
-
-    def gather_copy(side):
-        return remote(
-            q_own,
-            gathered.at[side],
-            gather_send.at[side],
-            gather_recv.at[side],
-            ring_device(away[side]),
-        )
-
-    wait_for(q_own.at[0 : heads - 1], spread_recv.at[0])
-    self_q.wait()
-    for side in range(2):
-        gather_copy(side).start()
-
-    wait_for(state_all.at[0, 0 : heads - 1], spread_recv.at[1])
-    self_state.wait()
-    state_mine = state_all.at[ring]
-
-    def send_state_on(k, carry):
-        remote(
-            state_mine, state_mine, spread_send.at[3], spread_recv.at[3], ring_device(k)
-        ).start()
-        return carry
-
-    lax.fori_loop(1, n, send_state_on, 0)
-
     load_filter.wait()
 
     def own_taps(h, carry):
@@ -322,6 +302,36 @@
         return carry
 
     lax.fori_loop(0, heads, own_taps, 0)
+    taps_own[...] = jnp.transpose(filt_v[lanes_of(head), :])
+    state_rows[taps:, :] = jnp.zeros((positions, HEAD_DIM), F32)
+
+    away = (3, n - 3)
+
+    def gather_copy(side):
+        return remote(
+            q_own,
+            gathered.at[side],
+            gather_send.at[side],
+            gather_recv.at[side],
+            ring_device(away[side]),
+        )
+
+    wait_for(q_own.at[0 : heads - 1], spread_recv.at[0])
+    self_q.wait()
+    for side in range(2):
+        gather_copy(side).start()
+
+    wait_for(state_all.at[0, 0 : heads - 1], spread_recv.at[1])
+    self_state.wait()
+    state_mine = state_all.at[ring]
+
+    def send_state_on(k, carry):
+        remote(
+            state_mine, state_mine, spread_send.at[3], spread_recv.at[3], ring_device(k)
+        ).start()
+        return carry
+
+    farthest_first(send_state_on)
 
     right = ring_device(1)
     left = ring_device(n - 1)
@@ -347,8 +357,6 @@
     for copy in values_on:
         copy.start()
 
-    taps_own[...] = jnp.transpose(filt_v[lanes_of(head), :])
-    state_rows[taps:, :] = jnp.zeros((positions, HEAD_DIM), F32)
     wait_for(state_all.at[0 : n - 1], spread_recv.at[3])
 
     for at in range(n):
@@ -391,7 +399,7 @@
             state_back(back_device(k, core_to)[1]).start()
         return carry
 
-    lax.fori_loop(1, n, send_state_back, 0)
+    farthest_first(send_state_back)
     state_back(sibling).start()
     state_parts[head] = state_part[...]
 
@@ -496,6 +504,47 @@
     for place, first, last in spans[2]:
         store_sums(2, merge(load_sums(2), attend(chunk_of(2), place)))
 
+    mine = load_sums(2)
+    for side in range(2):
+        part_copy(side).wait_recv()
+        stat_copy(side).wait_recv()
+        mine = merge(
+            mine,
+            (part_in[side].astype(F32), stat_in[side, 0:1, :], stat_in[side, 1:2, :]),
+        )
+    numer, peak, total = mine
+    merged[...] = jnp.transpose(numer).astype(BF16).reshape(merged.shape)
+    for b in range(rows // HEAD_DIM):
+        merged_stat[b, 0:1, :] = peak[:, b * HEAD_DIM : (b + 1) * HEAD_DIM]
+        merged_stat[b, 1:2, :] = total[:, b * HEAD_DIM : (b + 1) * HEAD_DIM]
+
+    def back_copy(slot, device_id):
+        return remote(
+            merged.at[slot], back.at[head], back_send.at[1], back_recv.at[1], device_id
+        )
+
+    def back_stat_copy(slot, device_id):
+        return remote(
+            merged_stat.at[lax.div(slot, group)],
+            back_stat.at[head],
+            back_send.at[2],
+            back_recv.at[2],
+            device_id,
+        )
+
+    def send_back(k, carry):
+        for core_to in range(2):
+            slot, device_id = back_device(k, core_to)
+            back_copy(slot, device_id).start()
+            back_stat_copy(slot, device_id).start()
+        return carry
+
+    farthest_first(send_back)
+    back_copy(slot_beside, sibling).start()
+    back_stat_copy(slot_beside, sibling).start()
+    back[head] = merged[slot_self]
+    back_stat[head] = merged_stat[lax.div(slot_self, group)]
+
     wait_for(state_parts.at[0 : heads - 1], back_recv.at[0])
     for h in range(heads):
         lanes = slice(h * HEAD_DIM, (h + 1) * HEAD_DIM)
@@ -503,7 +552,6 @@
             hy_v[0, :, lanes].astype(F32) * (mixed[:, lanes] + state_parts[h].astype(F32))
         ).astype(BF16)
     load_keys.wait()
-    group = HEAD_DIM // positions
     own = []
     row_at = lax.broadcasted_iota(jnp.int32, (HEAD_DIM, HEAD_DIM), 0)
     col_at = lax.broadcasted_iota(jnp.int32, (HEAD_DIM, HEAD_DIM), 1)
@@ -527,47 +575,6 @@
             weights.astype(BF16), stacked(hyena_ref.at[0], g), preferred_element_type=F32
         )
         own.append((numer, top, total))
-
-    mine = load_sums(2)
-    for side in range(2):
-        part_copy(side).wait_recv()
-        stat_copy(side).wait_recv()
-        mine = merge(
-            mine,
-            (part_in[side].astype(F32), stat_in[side, 0:1, :], stat_in[side, 1:2, :]),
-        )
-    numer, peak, total = mine
-    merged[...] = jnp.transpose(numer).astype(BF16).reshape(merged.shape)
-    for b in range(rows // HEAD_DIM):
-        merged_stat[b, 0:1, :] = peak[:, b * HEAD_DIM : (b + 1) * HEAD_DIM]
-        merged_stat[b, 1:2, :] = total[:, b * HEAD_DIM : (b + 1) * HEAD_DIM]
-
-    def back_copy(slot, device_id):
-        return remote(
-            merged.at[slot], back.at[head], back_send.at[1], back_recv.at[1], device_id
-        )
-
-    def back_stat_copy(slot, device_id):
-        return remote(
-            merged_stat.at[lax.div(slot, group)],
-            back_stat.at[head],
-            back_send.at[2],
-            back_recv.at[2],
-            device_id,
-        )
-
-    def send_back(k, carry):
-        for core_to in range(2):
-            slot, device_id = back_device(k, core_to)
-            back_copy(slot, device_id).start()
-            back_stat_copy(slot, device_id).start()
-        return carry
-
-    lax.fori_loop(1, n, send_back, 0)
-    back_copy(slot_beside, sibling).start()
-    back_stat_copy(slot_beside, sibling).start()
-    back[head] = merged[slot_self]
-    back_stat[head] = merged_stat[lax.div(slot_self, group)]
 
     load_unembed.wait()
     stat_square[...] = jnp.zeros_like(stat_square)

time: 61.6 us -> 60.2 us (0.977)
  Pallas kernels: 55.2 us -> 54.4 us
    pallas_call x1, Pallas kernels: 55.2 us -> 54.4 us  [on_device(): pl.pallas_call(functools.partial(spread_kernel, n, tp_count), out_shape=(...]
where the time goes in v4:
time: 60.2 us; the launch traced here: 59.8 us
  Pallas kernels  54.4 us (90%)
  between operations  4.27 us (7%)
  local copies, waits for them, and re-layouts  1.17 us (2%)
    pallas_call x1, Pallas kernels, on_device(): pl.pallas_call(functools.partial(spread_kernel, n, tp_count), out_shape=(...  54.4 us

profile of v4, /device:TPU:1, one launch (start us, length us, event | category | flops | bytes accessed | tf_op | source)
XLA Modules:
  0.0 59.8 jit_solution(8664996029492800137)
XLA Ops:
  2.6 54.4 %shard_map.139 = (bf16[1,32,2048]{2,1,0:T(8,128)(2,1)S(1)}, f32[1,32]{1,0:T(1,128)S(1)}, f32[1,1]{1,0:T(1,128)}) custom-call(bf16[2,64,2048]{2,1,0:T(8,128)(2,1)} %kv_ref.1, bf16[1,32,2048]{2,1,0:T(8,128)(2,1)} %q_ref.1, bf16[1,32,2048]{2,1,0:T(8,128)(2,1)} %ck_ref.1, bf16[3,1,32,2048]{3,2,1,0:T(8,128)(2,1)} %hy_ref.1, bf16[1,2048]{1,0:T(2,128)(2,1)} %state_ref.1, ...), custom_call_target="tpu_custom_call" | custom-call | tf_op jit(solution)/shard_map/pallas_call | solution.py:756
  56.9 0.7 %copy.21 = bf16[1,32,2048]{2,1,0:T(8,128)(2,1)} copy(bf16[1,32,2048]{2,1,0:T(8,128)(2,1)S(1)} %get-tuple-element.12) | data formatting | bytes 262144
  57.6 0.5 copy.22
